TPU v7x, 32 devices: a whole 2x2x4 slice. The times are simulated.
32 devices in a mesh: groups: 2 (over x), stream: 8 (over z, y), section: 2 (over core).
Axes of the slice: x: 2, y: 2, z: 4, core: 2. Of those that a mesh axis runs over, the one named last changes fastest.
Arguments:
- new_frames: bfloat16 [256, 16, 1024], P(('groups', 'stream')), parts along dimension 0, may hold values from -6 to 6
- valid_counts: int32 [256], P('groups'), parts along dimension 0, may hold values from 1 to 16
- anchor: int32 [256], P('groups'), parts along dimension 0, may hold values from 0 to 127, as said below
- context_cache: bfloat16 [2, 256, 12, 2048], P('section', ('groups', 'stream')), parts along dimension 1, may hold values from -240 to 240
- conv_state: bfloat16 [2, 256, 30, 1024], P('section', ('groups', 'stream')), parts along dimension 1, may hold values from -6 to 6
- qkv_weight: bfloat16 [2, 1024, 3072], P('section'), may hold values from -0.1875 to 0.1875
- out_weight: bfloat16 [2, 1024, 1024], P('section'), may hold values from -0.1875 to 0.1875
- conv_weight: float32 [2, 31, 1024], P('section'), may hold values from -1 to 1
Outputs:
- layer_outputs: bfloat16 [2, 256, 16, 1024], P('section', ('groups', 'stream')), parts along dimension 1
There are 2 independent parts, one for each index of `groups`. A program takes and returns all parts, laid end to end along the dimension named above; an argument that names none is the same for every part. Nothing has to cross between parts.
Inputs may be any that keep to these rules, and one draw needn't show every extreme that they name: anchor is a permutation of the 128 slots. New slot j lies on host j // 16, old slot o on host o // 16. Exactly 7 streams leave each host and 7 arrive at it; from one old host to one other new host moves at most one stream. A stream that stays on its host keeps its slot.
All inputs are finite; a program needn't handle non-finite values.
Results may differ from a plain program's by a relative error of at most 0.0094.
Values may be sent and summed in bfloat16 or wider, within the bound.
A program may use at most 128 MiB of HBM per device.

v0:
```python
import jax
import jax.numpy as jnp
from jax import lax
from jax.sharding import PartitionSpec as P

HEADS = 16


def shifted(value, axis, steps):
    count = lax.axis_size(axis)
    leading, last = (max(0, -steps), min(count, count - steps))
    return lax.ppermute(value, axis, [(source, source + steps) for source in range(leading, last)])


def encoder_layer(inputs, valid_counts, context, conv_state, qkv_weight, out_weight, conv_weight):
    stream_count, frame_count, model_width = inputs.shape
    head_size = model_width // HEADS
    live_mask = jnp.arange(frame_count, dtype=jnp.int32)[None, :] < valid_counts[:, None]
    floats = inputs.astype(jnp.float32)
    centred = floats - jnp.mean(floats, axis=-1, keepdims=True)
    variance = jnp.mean(centred * centred, axis=-1, keepdims=True)
    normed = (centred * lax.rsqrt(variance + 1e-05)).astype(jnp.bfloat16)
    projected = jnp.dot(
        normed.reshape(-1, model_width), qkv_weight, preferred_element_type=jnp.float32
    )
    projected = projected.reshape(stream_count, frame_count, 3 * model_width)
    queries = (projected[:, :, :model_width] * head_size ** (-0.5)).astype(jnp.bfloat16)
    new_keys = projected[:, :, model_width : 2 * model_width].astype(jnp.bfloat16)
    new_values = projected[:, :, 2 * model_width :].astype(jnp.bfloat16)
    keys_all = jnp.concatenate([context[:, :, :model_width], new_keys], axis=1)
    values_all = jnp.concatenate([context[:, :, model_width:], new_values], axis=1)
    key_total = keys_all.shape[1]
    queries_split = queries.reshape(stream_count, frame_count, HEADS, head_size)
    keys_split = keys_all.reshape(stream_count, key_total, HEADS, head_size)
    values_split = values_all.reshape(stream_count, key_total, HEADS, head_size)
    scores = jnp.einsum(
        "bqhd,bkhd->bhqk", queries_split, keys_split, preferred_element_type=jnp.float32
    )
    key_mask = jnp.concatenate(
        [jnp.ones((stream_count, key_total - frame_count), dtype=bool), live_mask], axis=1
    )
    scores = jnp.where(key_mask[:, None, None, :], scores, jnp.float32(-1e30))
    top_score = jnp.max(scores, axis=-1, keepdims=True)
    exponent = jnp.exp(scores - top_score)
    softmax_weights = (exponent / jnp.sum(exponent, axis=-1, keepdims=True)).astype(jnp.bfloat16)
    attended = jnp.einsum(
        "bhqk,bkhd->bqhd", softmax_weights, values_split, preferred_element_type=jnp.float32
    )
    attended = attended.reshape(stream_count * frame_count, model_width).astype(jnp.bfloat16)
    mixed = jnp.dot(attended, out_weight, preferred_element_type=jnp.float32)
    residual_sum = floats + mixed.reshape(stream_count, frame_count, model_width)
    rounded = lax.optimization_barrier(residual_sum.astype(jnp.bfloat16))
    padded_input = jnp.concatenate([conv_state, rounded], axis=1).astype(jnp.float32)
    convolved = jnp.zeros((stream_count, frame_count, model_width), jnp.float32)
    for tap_index in range(conv_weight.shape[0]):
        convolved = (
            convolved
            + conv_weight[tap_index][None, None, :]
            * padded_input[:, tap_index : tap_index + frame_count, :]
        )
    output = (residual_sum + jax.nn.silu(convolved)) * live_mask[:, :, None].astype(jnp.float32)
    return output.astype(jnp.bfloat16)


def routing(anchor, own_index, local_count):
    stream_total = anchor.shape[0]
    every_slot = jnp.arange(stream_total, dtype=jnp.int32)
    newpos = jnp.sum(
        jnp.where(anchor[None, :] == every_slot[:, None], every_slot[None, :], 0), axis=1
    )
    mine_new = lax.dynamic_slice_in_dim(newpos, own_index * local_count, local_count)
    mine_old = lax.dynamic_slice_in_dim(anchor, own_index * local_count, local_count)
    return (mine_new // local_count, mine_old // local_count, mine_new, mine_old)


def pack_rows(rows, hosts, own_index, slot_total):
    places = jnp.where(hosts == own_index, slot_total, hosts)
    return jnp.zeros((slot_total,) + rows.shape[1:], rows.dtype).at[places].set(rows, mode="drop")


def pick_rows(buffer, local_rows, hosts, own_index, local_index):
    from_buffer = jnp.take(buffer, hosts, axis=0)
    from_local = jnp.take(local_rows, local_index, axis=0)
    staying = (hosts == own_index).reshape((-1,) + (1,) * (buffer.ndim - 1))
    return jnp.where(staying, from_local, from_buffer)


def run_sections(inputs, valid_counts, context, conv_state, qkv_weight, out_weight, conv_weight):
    local_count = inputs.shape[0]
    block_total = 1
    block_rows = local_count // block_total
    section_total = lax.axis_size("section")
    section_index = lax.axis_index("section")
    inbound = jnp.zeros((block_rows,) + inputs.shape[1:], jnp.bfloat16)
    result = jnp.zeros_like(inputs)
    turn_total = block_total + section_total - 1
    for turn_index in range(turn_total):
        own_block = turn_index - section_index
        first_row = jnp.clip(own_block, 0, block_total - 1) * block_rows
        layer_input = jnp.where(section_index == 0, inputs, inbound)
        produced = encoder_layer(
            layer_input, valid_counts, context, conv_state, qkv_weight, out_weight, conv_weight
        )
        active = (own_block >= 0) & (own_block < block_total)
        previous = result
        result = jnp.where(active, produced, previous)
        if turn_index + 1 < turn_total:
            inbound = shifted(produced, "section", 1)
    return result


def body(
    new_frames, valid_counts, anchor, context_cache, conv_state, qkv_weight, out_weight, conv_weight
):
    local_count = new_frames.shape[0]
    own_index = lax.axis_index("stream")
    slot_total = lax.axis_size("stream")
    context_here = context_cache[0]
    conv_here = conv_state[0]
    target_host, source_host, mine_new, mine_old = routing(anchor, own_index, local_count)
    old_local = jnp.clip(mine_old - own_index * local_count, 0, local_count - 1)
    outgoing = (
        pack_rows(context_here, target_host, own_index, slot_total),
        pack_rows(conv_here, target_host, own_index, slot_total),
    )
    got_context, got_conv = (
        lax.all_to_all(outgoing[0], "stream", split_axis=0, concat_axis=0, tiled=True),
        lax.all_to_all(outgoing[1], "stream", split_axis=0, concat_axis=0, tiled=True),
    )
    valid_here = lax.dynamic_slice_in_dim(valid_counts, own_index * local_count, local_count)
    context_new = pick_rows(got_context, context_here, source_host, own_index, old_local)
    conv_new = pick_rows(got_conv, conv_here, source_host, own_index, old_local)
    section_output = run_sections(
        new_frames, valid_here, context_new, conv_new, qkv_weight[0], out_weight[0], conv_weight[0]
    )
    return section_output[None]


def solution(mesh):
    return jax.shard_map(
        body,
        mesh=mesh,
        in_specs=(
            P(("groups", "stream"), None, None),
            P("groups"),
            P("groups"),
            P("section", ("groups", "stream"), None, None),
            P("section", ("groups", "stream"), None, None),
            P("section", None, None),
            P("section", None, None),
            P("section", None, None),
        ),
        out_specs=P("section", ("groups", "stream"), None, None),
        check_vma=False,
    )
```

profile of v0, /device:TPU:1, one launch (start us, length us, event | category | flops | bytes accessed | tf_op | source)
XLA Modules:
  0.0 129.4 jit_solution(17258690904083255207)
XLA Ops:
  3.7 3.0 %scatter_fusion = bf16[8,12,2048]{2,1,0:T(8,128)(2,1)} fusion(bf16[8,12,2048]{2,1,0:T(8,128)(2,1)} %broadcast_in_dim.124, s32[16]{0:T(128)S(1)} %compare_select_fusion, bf16[16,12,2048]{2,1,0:T(8,128)(2,1)S(1)} %bitcast.73), kind=kCustom, calls=%fused_computation.4 | custom fusion | bytes 2359360 | tf_op jit(solution)/shard_map/scatter | solution.py:78
  6.8 6.6 %all-to-all-start = ((bf16[8,12,2048]{2,1,0:T(8,128)(2,1)}), bf16[8,12,2048]{2,1,0:T(8,128)(2,1)S(1)}, u32[]{:S(2)}, u32[]{:S(2)}) async-start(bf16[8,12,2048]{2,1,0:T(8,128)(2,1)} %scatter_fusion), calls=%async_computation | async-start | bytes 1048576 | tf_op jit(solution)/shard_map/all_to_all | solution.py:127
  13.5 2.8 %gather_fusion = bf16[16,12,2048]{2,1,0:T(8,128)(2,1)} fusion(bf16[16,12,2048]{2,1,0:T(8,128)(2,1)} %bitcast.74, s32[1024]{0:T(1024)S(1)} %pad_clamp_fusion.1), kind=kCustom, calls=%fused_computation | custom fusion | bytes 1572928 | tf_op jit(solution)/shard_map/jit(_take)/gather | solution.py:83
  16.8 5.8 %fusion.132 = (bf16[16,16,3072]{2,1,0:T(8,128)(2,1)}, f32[16,16,3072]{2,1,0:T(8,128)S(1)}) fusion(bf16[1,1024,3072]{2,1,0:T(8,128)(2,1)} %param.13, f32[16,16]{1,0:T(8,128)S(1)} %add_rsqrt_fusion.1, f32[16,16]{1,0:T(8,128)S(1)} %broadcast_multiply_fusion.1, bf16[16,16,1024]{2,1,0:T(8,128)(2,1)S(1)} %copy-done.1, pred[]{:T(512)S(6)} %eq.14), kind=kOutput, calls=%fused_computation.239 | convolution fusion | flops 1612709888 | bytes 11536385 | tf_op jit(solution)/shard_map/dot_general | solution.py:23
  23.5 2.5 %reshape.164 = bf16[16,16,16,64]{3,2,1,0:T(8,128)(2,1)} reshape(bf16[16,16,1024]{2,1,0:T(8,128)(2,1)} %fusion.107) | data formatting | bytes 1048576 | tf_op jit(solution)/shard_map/reshape | solution.py:33
  26.1 2.7 %copy.89 = bf16[1,16,30,1024]{3,2,1,0:T(8,128)(2,1)} copy(bf16[1,16,30,1024]{3,1,2,0:T(8,128)(2,1)} %param.12) | data formatting | bytes 1966080 | tf_op args[4]
  28.9 2.8 %gather_fusion.2 = bf16[16,30,1024]{2,1,0:T(8,128)(2,1)} fusion(bf16[16,30,1024]{2,1,0:T(8,128)(2,1)} %bitcast.75, s32[1024]{0:T(1024)S(1)} %pad_clamp_fusion.1), kind=kCustom, calls=%fused_computation.2 | custom fusion | bytes 1966144 | tf_op jit(solution)/shard_map/jit(_take)/gather | solution.py:83
  32.6 3.3 %scatter_fusion.1 = bf16[8,30,1024]{2,1,0:T(8,128)(2,1)} fusion(bf16[8,30,1024]{2,1,0:T(8,128)(2,1)} %broadcast_in_dim.135, s32[16]{0:T(128)S(1)} %compare_select_fusion, bf16[16,30,1024]{2,1,0:T(8,128)(2,1)} %bitcast.76), kind=kCustom, calls=%fused_computation.5 | custom fusion | bytes 2949184 | tf_op jit(solution)/shard_map/scatter | solution.py:78
  36.0 2.3 %fusion.128 = (bf16[16,16,1024]{2,1,0:T(8,128)(2,1)}, bf16[16,16,1024]{2,1,0:T(8,128)(2,1)}) fusion(bf16[16,16,3072]{2,1,0:T(8,128)(2,1)} %get-tuple-element.52), kind=kLoop, calls=%fused_computation.235 | loop fusion | bytes 2097152 | tf_op jit(solution)/shard_map/slice | solution.py:28
  38.3 5.5 %all-to-all-start.1 = ((bf16[8,30,1024]{2,1,0:T(8,128)(2,1)}), bf16[8,30,1024]{2,1,0:T(8,128)(2,1)}, u32[]{:S(2)}, u32[]{:S(2)}) async-start(bf16[8,30,1024]{2,1,0:T(8,128)(2,1)} %scatter_fusion.1), calls=%async_computation.1 | async-start | bytes 1048576 | tf_op jit(solution)/shard_map/all_to_all | solution.py:128
  45.4 1.9 %select_select_fusion.1 = bf16[16,12,2048]{2,1,0:T(8,128)(2,1)S(1)} fusion(bf16[16,12,2048]{2,1,0:T(8,128)(2,1)} %gather_fusion.1, bf16[16,12,2048]{2,1,0:T(8,128)(2,1)} %gather_fusion, pred[16]{0:T(512)(128)(4,1)S(1)} %compare_and_fusion, pred[16]{0:T(512)(128)(4,1)S(1)} %get-tuple-element.9, pred[16]{0:T(512)(128)(4,1)S(1)} %get-tuple-element.50), kind=kLoop, calls=%fused_computation.195 | loop fusion | flops 1179648 | bytes 2359344 | tf_op jit(solution)/shard_map/jit(_where)/select_n | solution.py:85
  49.5 3.7 %reshape.226 = bf16[16,28,16,64]{3,2,1,0:T(8,128)(2,1)} reshape(bf16[16,28,1024]{2,1,0:T(8,128)(2,1)} %pad_maximum_fusion.5) | data formatting | bytes 1835008 | tf_op jit(solution)/shard_map/reshape | solution.py:34
  53.2 5.2 %fusion.133 = (f32[16,16,16]{2,1,0:T(8,128)}, f32[16,16,16,28]{3,2,1,0:T(8,128)}) fusion(pred[16,28]{1,0:T(8,128)(4,1)S(1)} %concatenate.23, bf16[16,28,16,64]{3,2,1,0:T(8,128)(2,1)} %reshape.226, bf16[16,16,16,64]{3,2,1,0:T(8,128)(2,1)} %reshape.164), kind=kOutput, calls=%fused_computation.240 | convolution fusion | flops 15024155 | bytes 1917376 | tf_op jit(solution)/shard_map/sub | solution.py:44
  58.3 2.3 %pad_maximum_fusion.3 = bf16[16,28,1024]{2,1,0:T(8,128)(2,1)} fusion(bf16[16,12,1024]{2,1,0:T(8,128)(2,1)S(1)} %get-tuple-element.16, bf16[16,16,1024]{2,1,0:T(8,128)(2,1)} %get-tuple-element.14), kind=kLoop, calls=%fused_computation.51 | loop fusion | flops 1835008 | bytes 1835008 | tf_op jit(solution)/shard_map/concatenate | solution.py:31
  60.6 3.8 %reshape.225 = bf16[16,28,16,64]{3,2,1,0:T(8,128)(2,1)} reshape(bf16[16,28,1024]{2,1,0:T(8,128)(2,1)} %pad_maximum_fusion.3) | data formatting | bytes 1835008 | tf_op jit(solution)/shard_map/reshape | solution.py:35
  64.4 2.9 %fusion.31 = bf16[16,16,16,64]{3,1,2,0:T(8,128)(2,1)S(1)} fusion(bf16[16,28,16,64]{3,2,1,0:T(8,128)(2,1)} %reshape.225, f32[16,16,16,28]{3,2,1,0:T(8,128)} %get-tuple-element.55, f32[16,16,16]{2,1,0:T(8,128)S(1)} %copy-done.15), kind=kOutput, calls=%fused_computation.45 | convolution fusion | flops 15171584 | bytes 1916928 | tf_op jit(solution)/shard_map/bhqk,bkhd->bqhd/dot_general | solution.py:46
  68.5 2.6 %convert_element_type.81 = bf16[16,16,1024]{2,1,0:T(8,128)(2,1)} reshape(bf16[16,16,16,64]{3,2,1,0:T(8,128)(2,1)} %copy.35) | data formatting | bytes 1048576 | tf_op jit(solution)/shard_map/convert_element_type | solution.py:49
  71.2 2.8 %fusion.134 = (bf16[16,16,1024]{2,1,0:T(8,128)(2,1)S(1)}, f32[16,16,1024]{2,1,0:T(8,128)}) fusion(bf16[16,16,1024]{2,1,0:T(8,128)(2,1)} %convert_element_type.81, bf16[1,1024,1024]{2,1,0:T(8,128)(2,1)S(1)} %copy-done, bf16[16,16,1024]{2,1,0:T(8,128)(2,1)S(1)} %copy-done.1, pred[]{:T(512)S(6)} %eq.14), kind=kOutput, calls=%fused_computation.241 | convolution fusion | flops 537919488 | bytes 4718593 | tf_op jit(solution)/shard_map/dot_general | solution.py:50
  73.9 2.6 %gather_fusion.3 = bf16[16,30,1024]{2,1,0:T(8,128)(2,1)} fusion(bf16[8,30,1024]{2,1,0:T(8,128)(2,1)} %all-to-all-done.1, s32[1024]{0:T(1024)S(1)} %pad_clamp_fusion), kind=kCustom, calls=%fused_computation.3 | custom fusion | bytes 1966144 | tf_op jit(solution)/shard_map/jit(_take)/gather | solution.py:82
  76.5 1.8 %select_select_fusion = bf16[16,30,1024]{2,1,0:T(8,128)(2,1)S(1)} fusion(bf16[16,30,1024]{2,1,0:T(8,128)(2,1)} %gather_fusion.3, bf16[16,30,1024]{2,1,0:T(8,128)(2,1)} %gather_fusion.2, pred[16]{0:T(512)(128)(4,1)S(1)} %compare_and_fusion, pred[16]{0:T(512)(128)(4,1)S(1)} %get-tuple-element.9, pred[16]{0:T(512)(128)(4,1)S(1)} %get-tuple-element.50), kind=kLoop, calls=%fused_computation.191 | loop fusion | flops 1474560 | bytes 2949168 | tf_op jit(solution)/shard_map/jit(_where)/select_n | solution.py:85
  79.3 5.4 %multiply_convert_fusion.1 = bf16[16,16,1024]{2,1,0:T(8,128)(2,1)S(1)} fusion(f32[16,16,1024]{2,1,0:T(8,128)} %get-tuple-element.57, f32[16,46,1024]{2,1,0:T(8,128)S(1)} %fusion.20, f32[16,16]{1,0:T(8,128)S(1)} %get-tuple-element.48, f32[1024]{0:T(1024)S(1)} %bitcast.97, f32[1024]{0:T(1024)S(1)} %bitcast.99, f32[1024]{0:T(1024)S(1)} %bitcast.103, ...), kind=kLoop, calls=%fused_computation.190 | loop fusion | flops 17825792 | bytes 34206720 | tf_op jit(solution)/shard_map/convert_element_type | solution.py:62
  86.3 2.8 %collective-permute-done = bf16[16,16,1024]{2,1,0:T(8,128)(2,1)} collective-permute-done((bf16[16,16,1024]{2,1,0:T(8,128)(2,1)S(1)}, bf16[16,16,1024]{2,1,0:T(8,128)(2,1)}, u32[]{:S(2)}, u32[]{:S(2)}) %collective-permute-start) | collective-permute-done | bytes 524320 | tf_op jit(solution)/shard_map/ppermute | solution.py:12
  90.6 6.4 %fusion.135 = (bf16[16,16,3072]{2,1,0:T(8,128)(2,1)S(1)}, f32[16,16,3072]{2,1,0:T(8,128)}) fusion(bf16[1,1024,3072]{2,1,0:T(8,128)(2,1)} %param.13, bf16[16,16,1024]{2,1,0:T(8,128)(2,1)S(1)} %get-tuple-element.6, f32[16,16]{1,0:T(8,128)S(1)} %add_rsqrt_fusion, f32[16,16]{1,0:T(8,128)S(1)} %broadcast_multiply_fusion), kind=kOutput, calls=%fused_computation.242 | convolution fusion | flops 1612447744 | bytes 11536384 | tf_op jit(solution)/shard_map/dot_general | solution.py:23
  98.2 2.1 %pad_maximum_fusion.2 = (bf16[16,28,1024]{2,1,0:T(8,128)(2,1)}, bf16[16,28,1024]{2,1,0:T(8,128)(2,1)}) fusion(bf16[16,12,1024]{2,1,0:T(8,128)(2,1)S(1)} %copy-done.8, bf16[16,16,1024]{2,1,0:T(8,128)(2,1)S(1)} %get-tuple-element.12, bf16[16,16,1024]{2,1,0:T(8,128)(2,1)S(1)} %get-tuple-element.11, bf16[16,12,1024]{2,1,0:T(8,128)(2,1)S(1)} %copy-done.6), kind=kLoop, calls=%fused_computation.50 | loop fusion | flops 3670016 | bytes 3670016 | tf_op jit(solution)/shard_map/concatenate | solution.py:31
  100.2 3.8 %reshape.228 = bf16[16,28,16,64]{3,2,1,0:T(8,128)(2,1)} reshape(bf16[16,28,1024]{2,1,0:T(8,128)(2,1)} %get-tuple-element.65) | data formatting | bytes 1835008 | tf_op jit(solution)/shard_map/reshape | solution.py:34
  105.3 1.7 %reshape.167 = bf16[16,16,16,64]{3,2,1,0:T(8,128)(2,1)} reshape(bf16[16,16,1024]{2,1,0:T(8,128)(2,1)S(1)} %fusion.76) | data formatting | bytes 1048576 | tf_op jit(solution)/shard_map/reshape | solution.py:33
  107.0 3.8 %reshape.227 = bf16[16,28,16,64]{3,2,1,0:T(8,128)(2,1)} reshape(bf16[16,28,1024]{2,1,0:T(8,128)(2,1)} %get-tuple-element.64) | data formatting | bytes 1835008 | tf_op jit(solution)/shard_map/reshape | solution.py:35
  110.7 4.5 %fusion.136 = (f32[16,16,16]{2,1,0:T(8,128)S(1)}, f32[16,16,16,28]{3,2,1,0:T(8,128)}) fusion(pred[16,28]{1,0:T(8,128)(4,1)S(1)} %concatenate.23, bf16[16,28,16,64]{3,2,1,0:T(8,128)(2,1)} %reshape.228, bf16[16,16,16,64]{3,2,1,0:T(8,128)(2,1)} %reshape.167), kind=kOutput, calls=%fused_computation.243 | convolution fusion | flops 15024155 | bytes 1917376 | tf_op jit(solution)/shard_map/sub | solution.py:44
  115.2 2.9 %fusion.28 = bf16[16,16,16,64]{3,1,2,0:T(8,128)(2,1)S(1)} fusion(bf16[16,28,16,64]{3,2,1,0:T(8,128)(2,1)} %reshape.227, f32[16,16,16,28]{3,2,1,0:T(8,128)} %get-tuple-element.61, f32[16,16,16]{2,1,0:T(8,128)S(1)} %get-tuple-element.60), kind=kOutput, calls=%fused_computation.44 | convolution fusion | flops 15171584 | bytes 1916928 | tf_op jit(solution)/shard_map/bhqk,bkhd->bqhd/dot_general | solution.py:46
  119.4 1.9 %convert_element_type.92 = bf16[16,16,1024]{2,1,0:T(8,128)(2,1)S(1)} reshape(bf16[16,16,16,64]{3,2,1,0:T(8,128)(2,1)} %copy.42) | data formatting | bytes 1048576 | tf_op jit(solution)/shard_map/convert_element_type | solution.py:49
  121.3 1.7 %fusion.137 = (bf16[16,16,1024]{2,1,0:T(8,128)(2,1)S(1)}, f32[16,16,1024]{2,1,0:T(8,128)}) fusion(bf16[16,16,1024]{2,1,0:T(8,128)(2,1)S(1)} %convert_element_type.92, bf16[1,1024,1024]{2,1,0:T(8,128)(2,1)S(1)} %copy-done, bf16[16,16,1024]{2,1,0:T(8,128)(2,1)S(1)} %get-tuple-element.6), kind=kOutput, calls=%fused_computation.244 | convolution fusion | flops 537657344 | bytes 4718592 | tf_op jit(solution)/shard_map/dot_general | solution.py:50
  124.2 5.1 %select_bitcast_fusion = bf16[1,16,16,1024]{3,2,1,0:T(8,128)(2,1)} fusion(bf16[16,16,1024]{2,1,0:T(8,128)(2,1)} %copy-done.10, pred[]{:T(512)S(6)} %and.36, pred[]{:T(512)S(6)} %and.31, f32[16,16]{1,0:T(8,128)S(1)} %get-tuple-element.48, f32[16,16,1024]{2,1,0:T(8,128)S(1)} %copy-done.9, f32[16,46,1024]{2,1,0:T(8,128)S(1)} %fusion.21, f32[1024]{0:T(1024)S(1)} %bitcast.98, ...), kind=kLoop, calls=%fused_computation.198 | loop fusion | flops 18350080 | bytes 34731008 | tf_op jit(solution)/shard_map/broadcast_in_dim | solution.py:136
  (68 shorter events, 20.3 us)
Async XLA Ops:
  0.0 71.2 %copy-start = (bf16[1,1024,1024]{2,1,0:T(8,128)(2,1)S(1)}, bf16[1,1024,1024]{2,1,0:T(8,128)(2,1)}, u32[]{:S(2)}) copy-start(bf16[1,1024,1024]{2,1,0:T(8,128)(2,1)} %param.14) | copy-start | bytes 6291460
  2.5 1.2 copy-start.2
  3.7 9.6 %copy-start.13 = (s32[128]{0:T(128)S(1)}, s32[128]{0:T(128)}, u32[]{:S(2)}) copy-start(s32[128]{0:T(128)} %param.10) | copy-start | bytes 1540
  6.8 9.5 %copy-start.1 = (bf16[16,16,1024]{2,1,0:T(8,128)(2,1)S(1)}, bf16[16,16,1024]{2,1,0:T(8,128)(2,1)}, u32[]{:S(2)}) copy-start(bf16[16,16,1024]{2,1,0:T(8,128)(2,1)} %param.8) | copy-start | bytes 1572868
  6.8 31.6 %all-to-all-start = ((bf16[8,12,2048]{2,1,0:T(8,128)(2,1)}), bf16[8,12,2048]{2,1,0:T(8,128)(2,1)S(1)}, u32[]{:S(2)}, u32[]{:S(2)}) async-start(bf16[8,12,2048]{2,1,0:T(8,128)(2,1)} %scatter_fusion), calls=%async_computation | async-start | bytes 1048576 | tf_op jit(solution)/shard_map/all_to_all | solution.py:127
  22.6 3.4 %copy-start.14 = (s32[128]{0:T(128)S(1)}, s32[128]{0:T(128)}, u32[]{:S(2)}) copy-start(s32[128]{0:T(128)} %param.9) | copy-start | bytes 1540
  31.7 4.2 %copy-start.12 = (f32[1,31,1024]{2,0,1:T(1,128)S(1)}, f32[1,31,1024]{2,0,1:T(1,128)}, u32[]{:S(2)}) copy-start(f32[1,31,1024]{2,0,1:T(1,128)} %param.15) | copy-start | bytes 380932
  38.3 35.6 %all-to-all-start.1 = ((bf16[8,30,1024]{2,1,0:T(8,128)(2,1)}), bf16[8,30,1024]{2,1,0:T(8,128)(2,1)}, u32[]{:S(2)}, u32[]{:S(2)}) async-start(bf16[8,30,1024]{2,1,0:T(8,128)(2,1)} %scatter_fusion.1), calls=%async_computation.1 | async-start | bytes 1048576 | tf_op jit(solution)/shard_map/all_to_all | solution.py:128
  45.4 2.8 %copy-start.11 = (bf16[16,16,1024]{2,1,0:T(8,128)(2,1)S(1)}, bf16[16,16,1024]{2,1,0:T(8,128)(2,1)}, u32[]{:S(2)}) copy-start(bf16[16,16,1024]{2,1,0:T(8,128)(2,1)} %get-tuple-element.13) | copy-start | bytes 1572868
  47.4 0.8 copy-start.5
  47.4 11.0 %copy-start.7 = (bf16[16,12,1024]{2,1,0:T(8,128)(2,1)}, bf16[16,12,1024]{2,1,0:T(8,128)(2,1)S(1)}, u32[]{:S(2)}) copy-start(bf16[16,12,1024]{2,1,0:T(8,128)(2,1)S(1)} %get-tuple-element.16) | copy-start | bytes 1179652
  60.6 3.8 %copy-start.15 = (f32[16,16,16]{2,1,0:T(8,128)S(1)}, f32[16,16,16]{2,1,0:T(8,128)}, u32[]{:S(2)}) copy-start(f32[16,16,16]{2,1,0:T(8,128)} %get-tuple-element.54) | copy-start | bytes 49156
  78.4 1.0 copy-start.3
  84.7 1.5 %copy-start.10 = (bf16[16,16,1024]{2,1,0:T(8,128)(2,1)}, bf16[16,16,1024]{2,1,0:T(8,128)(2,1)S(1)}, u32[]{:S(2)}) copy-start(bf16[16,16,1024]{2,1,0:T(8,128)(2,1)S(1)} %multiply_convert_fusion.1) | copy-start | bytes 1572868
  84.7 4.3 %collective-permute-start = (bf16[16,16,1024]{2,1,0:T(8,128)(2,1)S(1)}, bf16[16,16,1024]{2,1,0:T(8,128)(2,1)}, u32[]{:S(2)}, u32[]{:S(2)}) collective-permute-start(bf16[16,16,1024]{2,1,0:T(8,128)(2,1)S(1)} %multiply_convert_fusion.1), channel_id=1, source_target_pairs={{0,1},{2,3},{4,5},{6,7},{8,9},{10,11},{12,13},{14,15},{16,17},{18,... | collective-permute-start | bytes 1572872 | tf_op jit(solution)/shard_map/ppermute | solution.py:12
  97.0 1.0 copy-start.6
  97.0 1.2 copy-start.8
  121.3 1.7 %copy-start.4 = (bf16[16,30,1024]{2,1,0:T(8,128)(2,1)S(1)}, bf16[16,30,1024]{2,1,0:T(8,128)(2,1)}, u32[]{:S(2)}) copy-start(bf16[16,30,1024]{2,1,0:T(8,128)(2,1)} %copy-done.3) | copy-start | bytes 2949124
  123.0 1.2 copy-start.9
where the time goes:
time: 131 us; the launch traced here: 129 us
  local copies, waits for them, and re-layouts  54.7 us (42%)
  matrix products  32 us (24%)
  other arithmetic  26.1 us (20%)
  starting transfers between devices  13.6 us (10%)
  waiting for transfers between devices  2.79 us (2%)
    dot_general x2, matrix products, encoder_layer(): jnp.dot(normed.reshape(-1, model_width), qkv_weight, preferred_element_ty...  12.2 us
    sub x2, matrix products, encoder_layer(): exponent = jnp.exp(scores - top_score)  9.65 us
    unnamed x34, local copies, waits for them, and re-layouts  7.75 us
    reshape x2, local copies, waits for them, and re-layouts, encoder_layer(): values_split = values_all.reshape(stream_count, key_total, HEADS, head_size)  7.54 us
    reshape x2, local copies, waits for them, and re-layouts, encoder_layer(): keys_split = keys_all.reshape(stream_count, key_total, HEADS, head_size)  7.5 us
    convert_element_type x4, local copies, waits for them, and re-layouts, encoder_layer(): attended.reshape(stream_count * frame_count, model_width)  7.05 us
    all_to_all x1, starting transfers between devices, body(): lax.all_to_all(outgoing[0], 'stream', split_axis=0, concat_axis=0, tiled=...  6.58 us
    scatter x2, local copies, waits for them, and re-layouts, pack_rows(): jnp.zeros((slot_total,) + rows.shape[1:], rows.dtype).at[places]  6.36 us
  transfers between devices with their start and end apart: 3, of which 1 were waited for; matrix products, arithmetic and copies ran while one was open for 42% of the time, Pallas kernels for 0%

commit v1 on v0

v1 whole, which is shorter than its diff:
```python
import functools

import jax
import jax.numpy as jnp
from jax import lax
from jax.experimental import pallas as pl
from jax.experimental.pallas import tpu as pltpu
from jax.sharding import PartitionSpec as P

HEADS = 16
CHUNK = 8
MESH = pl.DeviceIdType.MESH


def kernel(
    hosts, streams, frames, width, ctx_rows, kept_rows, taps,
    anchor, valid, x_hbm, ctx_hbm, kept_hbm, wqkv_hbm, wout_hbm, wconv_hbm, out_ref,
    x_v, ctx_v, kept_v, wqkv, wout, wconv,
    x_send, x_recv, y_send, y_recv, x_work, y_work,
    normed, q_buf, k_buf, v_buf, att_buf, bias, res_buf, pad_t, conv_t,
    t_send, t_old, rank, perm, host_of, count_of,
    load_sem, xs_sem, xr_sem, ys_sem, yr_sem, hs_sem, hr_sem,
):
    me = lax.axis_index("stream")
    section = lax.axis_index("section")
    base = me * streams
    rows = CHUNK * frames
    chunks = streams // CHUNK
    group = 4
    half = group * frames
    lanes = 128

    loads = [
        pltpu.make_async_copy(x_hbm, x_v, load_sem.at[0]),
        pltpu.make_async_copy(kept_hbm.at[0], kept_v, load_sem.at[1]),
        pltpu.make_async_copy(ctx_hbm.at[0], ctx_v, load_sem.at[2]),
        pltpu.make_async_copy(wconv_hbm.at[0], wconv, load_sem.at[3]),
        pltpu.make_async_copy(wqkv_hbm.at[0], wqkv, load_sem.at[4]),
        pltpu.make_async_copy(wout_hbm.at[0], wout, load_sem.at[5]),
    ]
    for load in loads:
        load.start()

    barrier = pltpu.get_barrier_semaphore()

    def greet(step, _):
        pl.semaphore_signal(
            barrier, inc=1, device_id={"stream": lax.rem(me + step, hosts)}, device_id_type=MESH
        )
        return 0

    lax.fori_loop(1, hosts, greet, 0)
    pl.semaphore_signal(barrier, inc=1, device_id={"section": 1 - section}, device_id_type=MESH)

    def scan_send(h, _):
        found = jnp.int32(0)
        for i in range(streams):
            found = jnp.where(anchor[base + i] // streams == h, i, found)
        t_send[h] = found
        return 0

    lax.fori_loop(0, hosts, scan_send, 0)
    loads[0].wait()
    pl.semaphore_wait(barrier, hosts)

    def x_copy(to):
        return pltpu.make_async_remote_copy(
            src_ref=x_send.at[to], dst_ref=x_recv.at[me],
            send_sem=xs_sem.at[to], recv_sem=xr_sem.at[me],
            device_id={"stream": to}, device_id_type=MESH,
        )

    def x_arrival(source):
        return pltpu.make_async_remote_copy(
            src_ref=x_send.at[source], dst_ref=x_recv.at[source],
            send_sem=xs_sem.at[source], recv_sem=xr_sem.at[source],
            device_id={"stream": source}, device_id_type=MESH,
        )

    def y_copy(to):
        return pltpu.make_async_remote_copy(
            src_ref=y_send.at[to], dst_ref=y_recv.at[me],
            send_sem=ys_sem.at[to], recv_sem=yr_sem.at[me],
            device_id={"stream": to}, device_id_type=MESH,
        )

    def y_arrival(source):
        return pltpu.make_async_remote_copy(
            src_ref=y_send.at[source], dst_ref=y_recv.at[source],
            send_sem=ys_sem.at[source], recv_sem=yr_sem.at[source],
            device_id={"stream": source}, device_id_type=MESH,
        )

    def hand_over(chunk):
        span = pl.ds(chunk * CHUNK, CHUNK)
        return pltpu.make_async_remote_copy(
            src_ref=y_work.at[span], dst_ref=x_work.at[span],
            send_sem=hs_sem.at[chunk], recv_sem=hr_sem.at[chunk],
            device_id={"section": 1 - section}, device_id_type=MESH,
        )

    @pl.when(section == 0)
    def _():
        def send(step, _):
            to = lax.rem(me + step, hosts)
            x_send[to] = x_v[t_send[to]]
            x_copy(to).start()
            return 0

        lax.fori_loop(1, hosts, send, 0)

    def scan_old(h, _):
        found = jnp.int32(-1)
        for i in range(streams):
            slot = anchor[h * streams + i]
            found = jnp.where(slot // streams == me, slot - base, found)
        t_old[h] = jnp.where(h == me, -1, found)
        return 0

    lax.fori_loop(0, hosts, scan_old, 0)
    stays = [anchor[base + i] // streams == me for i in range(streams)]
    moved = jnp.int32(0)
    for i in range(streams):
        moved = moved + jnp.where(stays[i], 0, 1)
    gone, left = jnp.int32(0), moved
    for i in range(streams):
        rank[i] = jnp.where(stays[i], left, gone)
        left = left + jnp.where(stays[i], 1, 0)
        gone = gone + jnp.where(stays[i], 0, 1)

    def scan_perm(k, _):
        old = jnp.int32(0)
        for i in range(streams):
            old = jnp.where(rank[i] == k, i, old)
        perm[k] = old

        def scan_host(h, found):
            return jnp.where(t_old[h] == old, h, found)

        source = lax.fori_loop(0, hosts, scan_host, me)
        host_of[k] = source

        def scan_count(i, found):
            slot = source * streams + i
            return jnp.where(anchor[slot] == base + old, valid[slot], found)

        count_of[k] = lax.fori_loop(0, streams, scan_count, jnp.int32(0))
        return 0

    lax.fori_loop(0, streams, scan_perm, 0)

    loads[2].wait()
    loads[1].wait()
    loads[3].wait()

    def place(k, _):
        old = perm[k]
        g = k // group
        at = pl.multiple_of(lax.rem(k, group) * frames, frames)
        cached = ctx_v[old]
        filler = jnp.zeros((frames - ctx_rows, 2 * width), cached.dtype)
        cached = jnp.concatenate([cached, filler], axis=0)
        k_buf[g, pl.ds(at, frames), :] = cached[:, :width]
        v_buf[g, pl.ds(at, frames), :] = cached[:, width:]
        chunk = k // CHUNK
        kept = kept_v[old].astype(jnp.float32)
        for w in range(width // lanes):
            pad_t[chunk, w, pl.ds(lax.rem(k, CHUNK), kept_rows, stride=CHUNK), :] = kept[
                :, w * lanes : (w + 1) * lanes
            ]
        return 0

    lax.fori_loop(0, streams, place, 0)

    def mask_group(g, _):
        row = lax.broadcasted_iota(jnp.int32, (2 * half, 2 * half), 0)
        col = lax.broadcasted_iota(jnp.int32, (2 * half, 2 * half), 1)
        col_stream = lax.rem(col // frames, group)
        limit = jnp.full((2 * half, 2 * half), ctx_rows, jnp.int32)
        for i in range(group):
            limit = jnp.where((col >= half) & (col_stream == i), count_of[g * group + i], limit)
        open_ = (lax.rem(row // frames, group) == col_stream) & (lax.rem(col, frames) < limit)
        bias[g] = jnp.where(open_, 0.0, -1e30)
        return 0

    lax.fori_loop(0, streams // group, mask_group, 0)

    def conv_kept(step, _):
        chunk = step // (width // lanes)
        w = lax.rem(step, width // lanes)
        at = pl.ds(pl.multiple_of(w * lanes, lanes), lanes)
        total = jnp.zeros((rows, lanes), jnp.float32)
        for j in range(kept_rows):
            n = min(frames, kept_rows - j) * CHUNK
            term = wconv[pl.ds(j, 1), at] * pad_t[chunk, w, pl.ds(j * CHUNK, n), :]
            if n < rows:
                total = jnp.concatenate([total[:n] + term, total[n:]], axis=0)
            else:
                total = total + term
        conv_t[chunk, w] = total
        return 0

    lax.fori_loop(0, chunks * (width // lanes), conv_kept, 0)

    def project(chunk):
        x = x_work[pl.ds(chunk * CHUNK, CHUNK)].reshape(rows, width).astype(jnp.float32)
        centred = x - jnp.mean(x, axis=-1, keepdims=True)
        variance = jnp.mean(centred * centred, axis=-1, keepdims=True)
        normed[...] = (centred * lax.rsqrt(variance + 1e-05)).astype(jnp.bfloat16)
        tile = 512

        def step_of(part):
            def step(i, _):
                at = pl.multiple_of(i * tile, tile)
                got = jnp.dot(
                    normed[...], wqkv[:, pl.ds(part * width + at, tile)],
                    preferred_element_type=jnp.float32,
                )
                if part == 0:
                    q_buf[chunk, :, pl.ds(at, tile)] = (
                        got * (width // HEADS) ** (-0.5)
                    ).astype(jnp.bfloat16)
                else:
                    got = got.astype(jnp.bfloat16)
                    to = k_buf if part == 1 else v_buf
                    for g in range(CHUNK // group):
                        to[chunk * (CHUNK // group) + g, pl.ds(half, half), pl.ds(at, tile)] = got[
                            g * half : (g + 1) * half
                        ]
                return 0

            return step

        for part in range(3):
            lax.fori_loop(0, width // tile, step_of(part), 0)

    def finish(chunk):
        def attend(g, _):
            lane = lax.broadcasted_iota(jnp.int32, (half, lanes), 1)
            first = lane < lanes // 2
            whole = chunk * (CHUNK // group) + g
            at_rows = pl.ds(pl.multiple_of(g * half, half), half)
            mask = bias[whole]

            def pair(p, _):
                at = pl.ds(pl.multiple_of(p * lanes, lanes), lanes)
                q = q_buf[chunk, at_rows, at]
                none = jnp.zeros_like(q)
                q = jnp.concatenate([jnp.where(first, q, none), jnp.where(first, none, q)], axis=0)
                scores = lax.dot_general(
                    q, k_buf[whole, :, at], (((1,), (1,)), ((), ())),
                    preferred_element_type=jnp.float32,
                ) + mask
                power = jnp.exp(scores - jnp.max(scores, axis=-1, keepdims=True))
                weights = power / jnp.sum(power, axis=-1, keepdims=True)
                mixed = jnp.dot(
                    weights.astype(jnp.bfloat16), v_buf[whole, :, at],
                    preferred_element_type=jnp.float32,
                )
                att_buf[at_rows, at] = jnp.where(first, mixed[:half], mixed[half:]).astype(
                    jnp.bfloat16
                )
                return 0

            lax.fori_loop(0, width // lanes, pair, 0, unroll=True)
            return 0

        lax.fori_loop(0, CHUNK // group, attend, 0)
        tile = 256

        def mix(i, _):
            at = pl.ds(pl.multiple_of(i * tile, tile), tile)
            got = jnp.dot(att_buf[...], wout[:, at], preferred_element_type=jnp.float32)
            x = x_work[pl.ds(chunk * CHUNK, CHUNK), :, at].reshape(rows, tile)
            res_buf[:, at] = x.astype(jnp.float32) + got
            return 0

        lax.fori_loop(0, width // tile, mix, 0)

        def spread(s, _):
            own = res_buf[pl.ds(pl.multiple_of(s * frames, frames), frames), :]
            own = own.astype(jnp.bfloat16).astype(jnp.float32)
            for w in range(width // lanes):
                pad_t[chunk, w, pl.ds(kept_rows * CHUNK + s, frames, stride=CHUNK), :] = own[
                    :, w * lanes : (w + 1) * lanes
                ]
            return 0

        lax.fori_loop(0, CHUNK, spread, 0)

        def conv_new(step, _):
            at = pl.ds(pl.multiple_of(step * lanes, lanes), lanes)
            total = conv_t[chunk, step]
            for j in range(taps - frames, taps):
                start = (kept_rows - j) * CHUNK
                n = rows - start
                term = wconv[pl.ds(j, 1), at] * pad_t[chunk, step, pl.ds(kept_rows * CHUNK, n), :]
                if start:
                    total = jnp.concatenate([total[:start], total[start:] + term], axis=0)
                else:
                    total = total + term
            conv_t[chunk, step] = total / (1.0 + jnp.exp(-total))
            return 0

        lax.fori_loop(0, width // lanes, conv_new, 0)

        def close(s, _):
            k = chunk * CHUNK + s
            own = res_buf[pl.ds(pl.multiple_of(s * frames, frames), frames), :]
            own = own + jnp.concatenate(
                [
                    conv_t[chunk, w, pl.ds(s, frames, stride=CHUNK), :]
                    for w in range(width // lanes)
                ],
                axis=1,
            )
            frame = lax.broadcasted_iota(jnp.int32, (frames, width), 0)
            y_work[k] = jnp.where(frame < count_of[k], own, 0.0).astype(jnp.bfloat16)
            return 0

        lax.fori_loop(0, CHUNK, close, 0)

    @pl.when(section == 0)
    def _():
        def stayer(k, _):
            x_work[k] = x_v[perm[k]]
            return 0

        lax.fori_loop(CHUNK, streams, stayer, 0)

    loads[4].wait()

    @pl.when(section == 0)
    def _():
        project(1)

        def arrive(step, _):
            x_arrival(lax.rem(me + step, hosts)).wait_recv()
            return 0

        lax.fori_loop(1, hosts, arrive, 0)

        def mover(k, _):
            source = host_of[k]
            x_work[k] = jnp.where(source == me, x_v[perm[k]], x_recv[source])
            return 0

        lax.fori_loop(0, CHUNK, mover, 0)

    @pl.when(section == 1)
    def _():
        hand_over(0).wait_recv()

    project(0)
    loads[5].wait()
    finish(0)

    @pl.when(section == 0)
    def _():
        hand_over(0).start()

    def give_back(step, _):
        to = lax.rem(me + step, hosts)
        y_send[to] = y_work[rank[jnp.maximum(t_old[to], 0)]]
        y_copy(to).start()
        return 0

    lax.fori_loop(1, hosts, give_back, 0)

    @pl.when(section == 1)
    def _():
        hand_over(1).wait_recv()
        project(1)

    finish(1)

    @pl.when(section == 0)
    def _():
        hand_over(1).start()

    def returned(step, _):
        y_arrival(lax.rem(me + step, hosts)).wait_recv()
        return 0

    lax.fori_loop(1, hosts, returned, 0)

    def assemble(i, _):
        source = anchor[base + i] // streams
        out_ref[0, i] = jnp.where(source == me, y_work[rank[i]], y_recv[source])
        return 0

    lax.fori_loop(0, streams, assemble, 0)

    def sent(step, _):
        y_copy(lax.rem(me + step, hosts)).wait_send()
        return 0

    lax.fori_loop(1, hosts, sent, 0)

    @pl.when(section == 0)
    def _():
        def x_sent(step, _):
            x_copy(lax.rem(me + step, hosts)).wait_send()
            return 0

        lax.fori_loop(1, hosts, x_sent, 0)
        hand_over(0).wait_send()
        hand_over(1).wait_send()


def body(new_frames, valid, anchor, context, kept, wqkv, wout, wconv):
    streams, frames, width = new_frames.shape
    hosts = lax.axis_size("stream")
    ctx_rows, kept_rows, taps = context.shape[2], kept.shape[2], wconv.shape[1]
    assert streams == 2 * CHUNK and lax.axis_size("section") == 2
    assert frames == 16 and taps == kept_rows + 1
    chunks, groups = streams // CHUNK, streams // 4
    rows = CHUNK * frames
    bf16, f32, i32 = jnp.bfloat16, jnp.float32, jnp.int32
    vmem, smem = pltpu.VMEM, pltpu.SMEM
    dma = pltpu.SemaphoreType.DMA
    call = pl.pallas_call(
        functools.partial(kernel, hosts, streams, frames, width, ctx_rows, kept_rows, taps),
        out_shape=jax.ShapeDtypeStruct((1, streams, frames, width), bf16),
        in_specs=[pl.BlockSpec(memory_space=pltpu.SMEM)] * 2
        + [pl.BlockSpec(memory_space=pl.ANY)] * 6,
        out_specs=pl.BlockSpec(memory_space=pltpu.VMEM),
        scratch_shapes=[
            vmem((streams, frames, width), bf16),
            vmem((streams, ctx_rows, 2 * width), bf16),
            vmem((streams, kept_rows, width), bf16),
            vmem((width, 3 * width), bf16),
            vmem((width, width), bf16),
            vmem((taps, width), f32),
            vmem((hosts, frames, width), bf16),
            vmem((hosts, frames, width), bf16),
            vmem((hosts, frames, width), bf16),
            vmem((hosts, frames, width), bf16),
            vmem((streams, frames, width), bf16),
            vmem((streams, frames, width), bf16),
            vmem((rows, width), bf16),
            vmem((chunks, rows, width), bf16),
            vmem((groups, 8 * frames, width), bf16),
            vmem((groups, 8 * frames, width), bf16),
            vmem((rows, width), bf16),
            vmem((groups, 8 * frames, 8 * frames), f32),
            vmem((rows, width), f32),
            vmem((chunks, width // 128, (kept_rows + frames) * CHUNK, 128), f32),
            vmem((chunks, width // 128, rows, 128), f32),
            smem((hosts,), i32),
            smem((hosts,), i32),
            smem((streams,), i32),
            smem((streams,), i32),
            smem((streams,), i32),
            smem((streams,), i32),
            dma((6,)),
            dma((hosts,)),
            dma((hosts,)),
            dma((hosts,)),
            dma((hosts,)),
            dma((chunks,)),
            dma((chunks,)),
        ],
        compiler_params=pltpu.CompilerParams(
            collective_id=0, has_side_effects=True, vmem_limit_bytes=56 * 1024 * 1024
        ),
        cost_estimate=pl.CostEstimate(
            flops=2 * streams * frames * width * width * 4,
            bytes_accessed=12 * 1024 * 1024,
            transcendentals=streams * frames * width,
        ),
    )
    return call(anchor, valid, new_frames, context, kept, wqkv, wout, wconv)


def solution(mesh):
    return jax.shard_map(
        body,
        mesh=mesh,
        in_specs=(
            P(("groups", "stream"), None, None),
            P("groups"),
            P("groups"),
            P("section", ("groups", "stream"), None, None),
            P("section", ("groups", "stream"), None, None),
            P("section", None, None),
            P("section", None, None),
            P("section", None, None),
        ),
        out_specs=P("section", ("groups", "stream"), None, None),
        check_vma=False,
    )
```

time: 131 us -> 56.3 us (0.43); the launches traced: 129 us -> 56.1 us
  Pallas kernels: 0 us -> 47.2 us
  local copies, waits for them, and re-layouts: 54.7 us -> 8.82 us
  matrix products: 32 us -> 0 us
  other arithmetic: 26.1 us -> 0 us
  starting transfers between devices: 13.6 us -> 0 us
  waiting for transfers between devices: 2.79 us -> 0 us
    pallas_call x0 -> x1, Pallas kernels: none -> 47.2 us  [body(): return call(anchor, valid, new_frames, context, kept, wqkv, wout, wconv)]
    dot_general x6 -> x0, matrix products: 22.4 us -> none  [the longest x2 12.2 us: encoder_layer(): jnp.dot(normed.reshape(-1, model_width), qkv_weight, preferred_element_ty...]
    reshape x6 -> x0, local copies, waits for them, and re-layouts: 19.2 us -> none  [the longest x2 7.54 us: encoder_layer(): values_split = values_all.reshape(stream_count, key_total, HEADS, head_size)]
    all_to_all x2 -> x0, starting transfers between devices: 12 us -> none  [the longest x1 6.58 us: body(): lax.all_to_all(outgoing[0], 'stream', split_axis=0, concat_axis=0, tiled=...]
    gather x4 -> x0, local copies, waits for them, and re-layouts: 9.86 us -> none  [the longest x2 5.63 us: pick_rows(): from_local = jnp.take(local_rows, local_index, axis=0)]
    sub x2 -> x0, matrix products: 9.65 us -> none  [encoder_layer(): exponent = jnp.exp(scores - top_score)]
    convert_element_type x6 -> x0, other arithmetic: 8.48 us -> none  [the longest x1 5.36 us: encoder_layer(): return output.astype(jnp.bfloat16)]
    convert_element_type x4 -> x0, local copies, waits for them, and re-layouts: 7.05 us -> none  [encoder_layer(): attended.reshape(stream_count * frame_count, model_width)]
  transfers between devices with their start and end apart: 3 -> 0, of which waited for: 1 -> 0; matrix products, arithmetic and copies ran while one was open for 42% -> 0% of each run, Pallas kernels for 0% -> 0%
where the time goes in v1:
time: 56.3 us; the launch traced here: 56.1 us
  Pallas kernels  47.2 us (84%)
  local copies, waits for them, and re-layouts  8.82 us (16%)
    pallas_call x1, Pallas kernels, body(): return call(anchor, valid, new_frames, context, kept, wqkv, wout, wconv)  47.2 us
    unnamed x4, local copies, waits for them, and re-layouts  8.82 us

profile of v1, /device:TPU:1, one launch (start us, length us, event | category | flops | bytes accessed | tf_op | source)
XLA Modules:
  0.0 56.1 jit_solution(13540244853589796331)
XLA Ops:
  0.0 1.6 %copy.11.wconv_hbm = f32[1,31,1024]{2,1,0:T(8,128)} copy(f32[1,31,1024]{2,0,1:T(1,128)} %param.15) | data formatting | bytes 253952 | tf_op args[7]
  1.6 2.6 %copy.9.ctx_hbm = bf16[1,16,12,2048]{3,2,1,0:T(8,128)(2,1)} copy(bf16[1,16,12,2048]{3,1,2,0:T(8,128)(2,1)} %param.11) | data formatting | bytes 1572864 | tf_op args[3]
  4.2 2.8 %copy.10.kept_hbm = bf16[1,16,30,1024]{3,2,1,0:T(8,128)(2,1)} copy(bf16[1,16,30,1024]{3,1,2,0:T(8,128)(2,1)} %param.12) | data formatting | bytes 1966080 | tf_op args[4]
  6.9 47.2 %shard_map.82 = bf16[1,16,16,1024]{3,2,1,0:T(8,128)(2,1)} custom-call(s32[128]{0:T(128)} %anchor.1, s32[128]{0:T(128)} %valid.1, bf16[16,16,1024]{2,1,0:T(8,128)(2,1)} %x_hbm.1, bf16[1,16,12,2048]{3,2,1,0:T(8,128)(2,1)} %copy.9.ctx_hbm, bf16[1,16,30,1024]{3,2,1,0:T(8,128)(2,1)} %copy.10.kept_hbm, bf16[1,1024,3072]{2,1,0:T(8,128)(2,1)} %wqkv_hbm.1, ...), custom_call_target="tpu_custom_call" | custom-call | flops 2147483648 | bytes 12582912 | tf_op jit(solution)/shard_map/pallas_call | solution.py:473
  54.2 1.9 %copy.13 = bf16[1,16,16,1024]{3,2,1,0:T(8,128)(2,1)} copy(bf16[1,16,16,1024]{3,2,1,0:T(8,128)(2,1)} %shard_map.82) | data formatting | bytes 1048576

commit v2 on v1

--- a/solution.py
+++ b/solution.py
@@ -15,10 +15,10 @@
 def kernel(
     hosts, streams, frames, width, ctx_rows, kept_rows, taps,
     anchor, valid, x_hbm, ctx_hbm, kept_hbm, wqkv_hbm, wout_hbm, wconv_hbm, out_ref,
-    x_v, ctx_v, kept_v, wqkv, wout, wconv,
+    x_v, ctx_v, kept_v, wqkv, wout, wconv, pick, pick_kept,
     x_send, x_recv, y_send, y_recv, x_work, y_work,
     normed, q_buf, k_buf, v_buf, att_buf, bias, res_buf, pad_t, conv_t,
-    t_send, t_old, rank, perm, host_of, count_of,
+    t_send, t_old, t_count, rank, perm, host_of, count_of,
     load_sem, xs_sem, xr_sem, ys_sem, yr_sem, hs_sem, hr_sem,
 ):
     me = lax.axis_index("stream")
@@ -34,7 +34,7 @@
         pltpu.make_async_copy(x_hbm, x_v, load_sem.at[0]),
         pltpu.make_async_copy(kept_hbm.at[0], kept_v, load_sem.at[1]),
         pltpu.make_async_copy(ctx_hbm.at[0], ctx_v, load_sem.at[2]),
-        pltpu.make_async_copy(wconv_hbm.at[0], wconv, load_sem.at[3]),
+        pltpu.make_async_copy(wconv_hbm, wconv, load_sem.at[3]),
         pltpu.make_async_copy(wqkv_hbm.at[0], wqkv, load_sem.at[4]),
         pltpu.make_async_copy(wout_hbm.at[0], wout, load_sem.at[5]),
     ]
@@ -52,14 +52,19 @@
     lax.fori_loop(1, hosts, greet, 0)
     pl.semaphore_signal(barrier, inc=1, device_id={"section": 1 - section}, device_id_type=MESH)
 
+    shift = streams.bit_length() - 1
+    own = [anchor[base + i] for i in range(streams)]
+    own_host = [lax.shift_right_arithmetic(a, shift) for a in own]
+    short = hosts <= 8
+
     def scan_send(h, _):
         found = jnp.int32(0)
         for i in range(streams):
-            found = jnp.where(anchor[base + i] // streams == h, i, found)
+            found = jnp.where(own_host[i] == h, i, found)
         t_send[h] = found
         return 0
 
-    lax.fori_loop(0, hosts, scan_send, 0)
+    lax.fori_loop(0, hosts, scan_send, 0, unroll=short)
     loads[0].wait()
     pl.semaphore_wait(barrier, hosts)
 
@@ -110,97 +115,126 @@
         lax.fori_loop(1, hosts, send, 0)
 
     def scan_old(h, _):
-        found = jnp.int32(-1)
+        found, count = jnp.int32(-1), jnp.int32(0)
         for i in range(streams):
             slot = anchor[h * streams + i]
-            found = jnp.where(slot // streams == me, slot - base, found)
-        t_old[h] = jnp.where(h == me, -1, found)
-        return 0
-
-    lax.fori_loop(0, hosts, scan_old, 0)
-    stays = [anchor[base + i] // streams == me for i in range(streams)]
-    moved = jnp.int32(0)
+            hit = (lax.shift_right_arithmetic(slot, shift) == me) & (h != me)
+            found = jnp.where(hit, slot - base, found)
+            count = jnp.where(hit, valid[h * streams + i], count)
+        t_old[h] = found
+        t_count[h] = count
+        return 0
+
+    lax.fori_loop(0, hosts, scan_old, 0, unroll=short)
+    stays = [(h == me).astype(jnp.int32) for h in own_host]
+    moved = streams - sum(stays)
+    gone, left = jnp.int32(0), moved
+    ranks = []
     for i in range(streams):
-        moved = moved + jnp.where(stays[i], 0, 1)
-    gone, left = jnp.int32(0), moved
-    for i in range(streams):
-        rank[i] = jnp.where(stays[i], left, gone)
-        left = left + jnp.where(stays[i], 1, 0)
-        gone = gone + jnp.where(stays[i], 0, 1)
-
-    def scan_perm(k, _):
+        ranks.append(jnp.where(own_host[i] == me, left, gone))
+        rank[i] = ranks[i]
+        left = left + stays[i]
+        gone = gone + 1 - stays[i]
+    for k in range(streams):
         old = jnp.int32(0)
         for i in range(streams):
-            old = jnp.where(rank[i] == k, i, old)
+            old = jnp.where(ranks[i] == k, i, old)
         perm[k] = old
-
-        def scan_host(h, found):
-            return jnp.where(t_old[h] == old, h, found)
-
-        source = lax.fori_loop(0, hosts, scan_host, me)
-        host_of[k] = source
-
-        def scan_count(i, found):
-            slot = source * streams + i
-            return jnp.where(anchor[slot] == base + old, valid[slot], found)
-
-        count_of[k] = lax.fori_loop(0, streams, scan_count, jnp.int32(0))
-        return 0
-
-    lax.fori_loop(0, streams, scan_perm, 0)
+        count = valid[base + old]
+        if k < CHUNK:
+
+            def scan_host(h, found):
+                return jnp.where(t_old[h] == old, h, found)
+
+            source = lax.fori_loop(0, hosts, scan_host, me, unroll=short)
+            host_of[k] = source
+            count = jnp.where(source == me, count, t_count[source])
+        count_of[k] = count
 
     loads[2].wait()
     loads[1].wait()
     loads[3].wait()
 
-    def place(k, _):
-        old = perm[k]
-        g = k // group
-        at = pl.multiple_of(lax.rem(k, group) * frames, frames)
-        cached = ctx_v[old]
-        filler = jnp.zeros((frames - ctx_rows, 2 * width), cached.dtype)
-        cached = jnp.concatenate([cached, filler], axis=0)
-        k_buf[g, pl.ds(at, frames), :] = cached[:, :width]
-        v_buf[g, pl.ds(at, frames), :] = cached[:, width:]
-        chunk = k // CHUNK
-        kept = kept_v[old].astype(jnp.float32)
-        for w in range(width // lanes):
-            pad_t[chunk, w, pl.ds(lax.rem(k, CHUNK), kept_rows, stride=CHUNK), :] = kept[
-                :, w * lanes : (w + 1) * lanes
-            ]
-        return 0
-
-    lax.fori_loop(0, streams, place, 0)
-
-    def mask_group(g, _):
-        row = lax.broadcasted_iota(jnp.int32, (2 * half, 2 * half), 0)
-        col = lax.broadcasted_iota(jnp.int32, (2 * half, 2 * half), 1)
-        col_stream = lax.rem(col // frames, group)
+    span = ctx_rows * streams
+    row = lax.broadcasted_iota(jnp.int32, (frames, span), 0)
+    col = lax.broadcasted_iota(jnp.int32, (frames, span), 1)
+    slant = col - row * streams
+    for k in range(streams):
+        pick[pl.ds(k * frames, frames), :] = jnp.where(slant == perm[k], 1.0, 0.0).astype(
+            jnp.bfloat16
+        )
+
+    wide = 512
+
+    def place(i, _):
+        for part, to in enumerate((k_buf, v_buf)):
+            at = pl.multiple_of(i * wide, wide)
+            cached = ctx_v[:, :, pl.ds(part * width + at, wide)].reshape(span, wide)
+            cached = jnp.dot(pick[...], cached, preferred_element_type=jnp.float32)
+            cached = cached.astype(jnp.bfloat16)
+            for g in range(streams // group):
+                to[g, pl.ds(0, half), pl.ds(at, wide)] = cached[g * half : (g + 1) * half]
+        return 0
+
+    lax.fori_loop(0, width // wide, place, 0)
+
+    steps = 10
+    part_rows = steps * CHUNK
+    sub = lax.broadcasted_iota(jnp.int32, (CHUNK, steps * streams), 0)
+    col = lax.broadcasted_iota(jnp.int32, (CHUNK, steps * streams), 1)
+    blocks = []
+    for chunk in range(chunks):
+        wanted = jnp.zeros((CHUNK, steps * streams), jnp.int32)
+        for i in range(CHUNK):
+            wanted = jnp.where(sub == i, perm[chunk * CHUNK + i], wanted)
+        for t in range(steps):
+            blocks.append(jnp.where(col - t * streams == wanted, 1.0, 0.0))
+    pick_kept[...] = jnp.concatenate(blocks, axis=0).astype(jnp.bfloat16)
+
+    def place_kept(i, _):
+        at = pl.multiple_of(i * 2 * lanes, 2 * lanes)
+        for b in range(kept_rows // steps):
+            kept = kept_v[pl.ds(b * steps, steps), :, pl.ds(at, 2 * lanes)]
+            kept = kept.reshape(steps * streams, 2 * lanes)
+            kept = jnp.dot(pick_kept[...], kept, preferred_element_type=jnp.float32)
+            for chunk in range(chunks):
+                for w in range(2):
+                    pad_t[chunk, 2 * i + w, pl.ds(b * part_rows, part_rows), :] = kept[
+                        chunk * part_rows : (chunk + 1) * part_rows, w * lanes : (w + 1) * lanes
+                    ]
+        return 0
+
+    lax.fori_loop(0, width // (2 * lanes), place_kept, 0)
+
+    row = lax.broadcasted_iota(jnp.int32, (2 * half, 2 * half), 0)
+    col = lax.broadcasted_iota(jnp.int32, (2 * half, 2 * half), 1)
+    col_stream = lax.shift_right_arithmetic(col, frames.bit_length() - 1) & (group - 1)
+    same = lax.shift_right_arithmetic(row, frames.bit_length() - 1) & (group - 1) == col_stream
+    col_frame = col & (frames - 1)
+    for g in range(streams // group):
         limit = jnp.full((2 * half, 2 * half), ctx_rows, jnp.int32)
         for i in range(group):
             limit = jnp.where((col >= half) & (col_stream == i), count_of[g * group + i], limit)
-        open_ = (lax.rem(row // frames, group) == col_stream) & (lax.rem(col, frames) < limit)
-        bias[g] = jnp.where(open_, 0.0, -1e30)
-        return 0
-
-    lax.fori_loop(0, streams // group, mask_group, 0)
-
-    def conv_kept(step, _):
-        chunk = step // (width // lanes)
-        w = lax.rem(step, width // lanes)
-        at = pl.ds(pl.multiple_of(w * lanes, lanes), lanes)
-        total = jnp.zeros((rows, lanes), jnp.float32)
-        for j in range(kept_rows):
-            n = min(frames, kept_rows - j) * CHUNK
-            term = wconv[pl.ds(j, 1), at] * pad_t[chunk, w, pl.ds(j * CHUNK, n), :]
-            if n < rows:
-                total = jnp.concatenate([total[:n] + term, total[n:]], axis=0)
-            else:
-                total = total + term
-        conv_t[chunk, w] = total
-        return 0
-
-    lax.fori_loop(0, chunks * (width // lanes), conv_kept, 0)
+        bias[g] = jnp.where(same & (col_frame < limit), 0.0, -1e30)
+
+
+    def conv_kept(chunk):
+        def step(w, _):
+            at = pl.ds(pl.multiple_of(w * lanes, lanes), lanes)
+            total = jnp.zeros((rows, lanes), jnp.float32)
+            for j in range(kept_rows):
+                n = min(frames, kept_rows - j) * CHUNK
+                term = wconv[j, :, at] * pad_t[chunk, w, pl.ds(j * CHUNK, n), :]
+                if n < rows:
+                    total = jnp.concatenate([total[:n] + term, total[n:]], axis=0)
+                else:
+                    total = total + term
+            conv_t[chunk, w] = total
+            return 0
+
+        lax.fori_loop(0, width // lanes, step, 0)
+
+    conv_kept(0)
 
     def project(chunk):
         x = x_work[pl.ds(chunk * CHUNK, CHUNK)].reshape(rows, width).astype(jnp.float32)
@@ -252,7 +286,7 @@
                     preferred_element_type=jnp.float32,
                 ) + mask
                 power = jnp.exp(scores - jnp.max(scores, axis=-1, keepdims=True))
-                weights = power / jnp.sum(power, axis=-1, keepdims=True)
+                weights = power * (1.0 / jnp.sum(power, axis=-1, keepdims=True))
                 mixed = jnp.dot(
                     weights.astype(jnp.bfloat16), v_buf[whole, :, at],
                     preferred_element_type=jnp.float32,
@@ -294,7 +328,7 @@
             for j in range(taps - frames, taps):
                 start = (kept_rows - j) * CHUNK
                 n = rows - start
-                term = wconv[pl.ds(j, 1), at] * pad_t[chunk, step, pl.ds(kept_rows * CHUNK, n), :]
+                term = wconv[j, :, at] * pad_t[chunk, step, pl.ds(kept_rows * CHUNK, n), :]
                 if start:
                     total = jnp.concatenate([total[:start], total[start:] + term], axis=0)
                 else:
@@ -320,20 +354,10 @@
 
         lax.fori_loop(0, CHUNK, close, 0)
 
+    loads[4].wait()
+
     @pl.when(section == 0)
     def _():
-        def stayer(k, _):
-            x_work[k] = x_v[perm[k]]
-            return 0
-
-        lax.fori_loop(CHUNK, streams, stayer, 0)
-
-    loads[4].wait()
-
-    @pl.when(section == 0)
-    def _():
-        project(1)
-
         def arrive(step, _):
             x_arrival(lax.rem(me + step, hosts)).wait_recv()
             return 0
@@ -347,8 +371,15 @@
 
         lax.fori_loop(0, CHUNK, mover, 0)
 
+        def stayer(k, _):
+            x_work[k] = x_v[perm[k]]
+            return 0
+
+        lax.fori_loop(CHUNK, streams, stayer, 0)
+
     @pl.when(section == 1)
     def _():
+        conv_kept(1)
         hand_over(0).wait_recv()
 
     project(0)
@@ -367,11 +398,15 @@
 
     lax.fori_loop(1, hosts, give_back, 0)
 
+    @pl.when(section == 0)
+    def _():
+        conv_kept(1)
+
     @pl.when(section == 1)
     def _():
         hand_over(1).wait_recv()
-        project(1)
-
+
+    project(1)
     finish(1)
 
     @pl.when(section == 0)
@@ -385,7 +420,7 @@
     lax.fori_loop(1, hosts, returned, 0)
 
     def assemble(i, _):
-        source = anchor[base + i] // streams
+        source = lax.shift_right_arithmetic(anchor[base + i], shift)
         out_ref[0, i] = jnp.where(source == me, y_work[rank[i]], y_recv[source])
         return 0
 
@@ -412,8 +447,12 @@
     streams, frames, width = new_frames.shape
     hosts = lax.axis_size("stream")
     ctx_rows, kept_rows, taps = context.shape[2], kept.shape[2], wconv.shape[1]
+    context = jnp.transpose(context, (0, 2, 1, 3))
+    kept = jnp.transpose(kept, (0, 2, 1, 3))
+    wconv = jnp.transpose(wconv, (1, 0, 2))
     assert streams == 2 * CHUNK and lax.axis_size("section") == 2
-    assert frames == 16 and taps == kept_rows + 1
+    assert frames == 16 and taps == kept_rows + 1 and kept_rows % 10 == 0
+    assert streams & (streams - 1) == 0
     chunks, groups = streams // CHUNK, streams // 4
     rows = CHUNK * frames
     bf16, f32, i32 = jnp.bfloat16, jnp.float32, jnp.int32
@@ -427,11 +466,13 @@
         out_specs=pl.BlockSpec(memory_space=pltpu.VMEM),
         scratch_shapes=[
             vmem((streams, frames, width), bf16),
-            vmem((streams, ctx_rows, 2 * width), bf16),
-            vmem((streams, kept_rows, width), bf16),
+            vmem((ctx_rows, streams, 2 * width), bf16),
+            vmem((kept_rows, streams, width), bf16),
             vmem((width, 3 * width), bf16),
             vmem((width, width), bf16),
-            vmem((taps, width), f32),
+            vmem((taps, 1, width), f32),
+            vmem((streams * frames, ctx_rows * streams), bf16),
+            vmem((10 * streams, 10 * streams), bf16),
             vmem((hosts, frames, width), bf16),
             vmem((hosts, frames, width), bf16),
             vmem((hosts, frames, width), bf16),
@@ -447,6 +488,7 @@
             vmem((rows, width), f32),
             vmem((chunks, width // 128, (kept_rows + frames) * CHUNK, 128), f32),
             vmem((chunks, width // 128, rows, 128), f32),
+            smem((hosts,), i32),
             smem((hosts,), i32),
             smem((hosts,), i32),
             smem((streams,), i32),

time: 56.3 us -> 44.9 us (0.80)
  local copies, waits for them, and re-layouts: 8.82 us -> 1.88 us
  Pallas kernels: 47.2 us -> 42.8 us
    unnamed x4 -> x1, local copies, waits for them, and re-layouts: 8.82 us -> 1.88 us
    pallas_call x1, Pallas kernels: 47.2 us -> 42.8 us  [body(): return call(anchor, valid, new_frames, context, kept, wqkv, wout, wconv)]
where the time goes in v2:
time: 44.9 us; the launch traced here: 44.7 us
  Pallas kernels  42.8 us (95%)
  local copies, waits for them, and re-layouts  1.88 us (4%)
    pallas_call x1, Pallas kernels, body(): return call(anchor, valid, new_frames, context, kept, wqkv, wout, wconv)  42.8 us
    unnamed x1, local copies, waits for them, and re-layouts  1.88 us

profile of v2, /device:TPU:1, one launch (start us, length us, event | category | flops | bytes accessed | tf_op | source)
XLA Modules:
  0.0 44.7 jit_solution(7888594154399209266)
XLA Ops:
  0.0 42.8 %shard_map.82 = bf16[1,16,16,1024]{3,2,1,0:T(8,128)(2,1)} custom-call(s32[128]{0:T(128)} %anchor.1, s32[128]{0:T(128)} %valid.1, bf16[16,16,1024]{2,1,0:T(8,128)(2,1)} %x_hbm.1, bf16[1,12,16,2048]{3,2,1,0:T(8,128)(2,1)} %bitcast.4, bf16[1,30,16,1024]{3,2,1,0:T(8,128)(2,1)} %bitcast.3, bf16[1,1024,3072]{2,1,0:T(8,128)(2,1)} %wqkv_hbm.1, ...), custom_call_target="tpu_custom_call" | custom-call | flops 2147483648 | bytes 12582912 | tf_op jit(solution)/shard_map/pallas_call | solution.py:515
  42.8 1.9 %copy.10 = bf16[1,16,16,1024]{3,2,1,0:T(8,128)(2,1)} copy(bf16[1,16,16,1024]{3,2,1,0:T(8,128)(2,1)} %shard_map.82) | data formatting | bytes 1048576

commit v3 on v2

--- a/solution.py
+++ b/solution.py
@@ -17,7 +17,7 @@
     anchor, valid, x_hbm, ctx_hbm, kept_hbm, wqkv_hbm, wout_hbm, wconv_hbm, out_ref,
     x_v, ctx_v, kept_v, wqkv, wout, wconv, pick, pick_kept,
     x_send, x_recv, y_send, y_recv, x_work, y_work,
-    normed, q_buf, k_buf, v_buf, att_buf, bias, res_buf, pad_t, conv_t,
+    normed, q_buf, k_buf, v_buf, att_buf, s_buf, p_buf, bias, res_buf, pad_t, conv_t,
     t_send, t_old, t_count, rank, perm, host_of, count_of,
     load_sem, xs_sem, xr_sem, ys_sem, yr_sem, hs_sem, hr_sem,
 ):
@@ -241,7 +241,7 @@
         centred = x - jnp.mean(x, axis=-1, keepdims=True)
         variance = jnp.mean(centred * centred, axis=-1, keepdims=True)
         normed[...] = (centred * lax.rsqrt(variance + 1e-05)).astype(jnp.bfloat16)
-        tile = 512
+        tile = width
 
         def step_of(part):
             def step(i, _):
@@ -276,31 +276,31 @@
             at_rows = pl.ds(pl.multiple_of(g * half, half), half)
             mask = bias[whole]
 
-            def pair(p, _):
-                at = pl.ds(pl.multiple_of(p * lanes, lanes), lanes)
+            pairs = [pl.ds(p * lanes, lanes) for p in range(width // lanes)]
+            for p, at in enumerate(pairs):
                 q = q_buf[chunk, at_rows, at]
                 none = jnp.zeros_like(q)
                 q = jnp.concatenate([jnp.where(first, q, none), jnp.where(first, none, q)], axis=0)
-                scores = lax.dot_general(
+                s_buf[p] = lax.dot_general(
                     q, k_buf[whole, :, at], (((1,), (1,)), ((), ())),
                     preferred_element_type=jnp.float32,
-                ) + mask
-                power = jnp.exp(scores - jnp.max(scores, axis=-1, keepdims=True))
-                weights = power * (1.0 / jnp.sum(power, axis=-1, keepdims=True))
-                mixed = jnp.dot(
-                    weights.astype(jnp.bfloat16), v_buf[whole, :, at],
-                    preferred_element_type=jnp.float32,
                 )
-                att_buf[at_rows, at] = jnp.where(first, mixed[:half], mixed[half:]).astype(
+            for p, at in enumerate(pairs):
+                scores = s_buf[p] + mask
+                p_buf[p] = jnp.exp(scores - jnp.max(scores, axis=-1, keepdims=True)).astype(
                     jnp.bfloat16
                 )
-                return 0
-
-            lax.fori_loop(0, width // lanes, pair, 0, unroll=True)
+            ones = jnp.ones((2 * half, lanes), jnp.bfloat16)
+            for p, at in enumerate(pairs):
+                values = jnp.concatenate([v_buf[whole, :, at], ones], axis=1)
+                mixed = jnp.dot(p_buf[p], values, preferred_element_type=jnp.float32)
+                top = jnp.where(first, mixed[:half, :lanes], mixed[half:, :lanes])
+                total = jnp.where(first, mixed[:half, lanes:], mixed[half:, lanes:])
+                att_buf[at_rows, at] = (top / total).astype(jnp.bfloat16)
             return 0
 
         lax.fori_loop(0, CHUNK // group, attend, 0)
-        tile = 256
+        tile = width
 
         def mix(i, _):
             at = pl.ds(pl.multiple_of(i * tile, tile), tile)
@@ -320,7 +320,7 @@
                 ]
             return 0
 
-        lax.fori_loop(0, CHUNK, spread, 0)
+        lax.fori_loop(0, CHUNK, spread, 0, unroll=True)
 
         def conv_new(step, _):
             at = pl.ds(pl.multiple_of(step * lanes, lanes), lanes)
@@ -352,7 +352,7 @@
             y_work[k] = jnp.where(frame < count_of[k], own, 0.0).astype(jnp.bfloat16)
             return 0
 
-        lax.fori_loop(0, CHUNK, close, 0)
+        lax.fori_loop(0, CHUNK, close, 0, unroll=True)
 
     loads[4].wait()
 
@@ -484,6 +484,8 @@
             vmem((groups, 8 * frames, width), bf16),
             vmem((groups, 8 * frames, width), bf16),
             vmem((rows, width), bf16),
+            vmem((width // 128, 8 * frames, 8 * frames), f32),
+            vmem((width // 128, 8 * frames, 8 * frames), bf16),
             vmem((groups, 8 * frames, 8 * frames), f32),
             vmem((rows, width), f32),
             vmem((chunks, width // 128, (kept_rows + frames) * CHUNK, 128), f32),

time: 44.9 us -> 28 us (0.62)
  Pallas kernels: 42.8 us -> 26 us
    pallas_call x1, Pallas kernels: 42.8 us -> 26 us  [body(): return call(anchor, valid, new_frames, context, kept, wqkv, wout, wconv)]
where the time goes in v3:
time: 28 us; the launch traced here: 27.9 us
  Pallas kernels  26 us (93%)
  local copies, waits for them, and re-layouts  1.88 us (7%)
    pallas_call x1, Pallas kernels, body(): return call(anchor, valid, new_frames, context, kept, wqkv, wout, wconv)  26 us
    unnamed x1, local copies, waits for them, and re-layouts  1.88 us

profile of v3, /device:TPU:1, one launch (start us, length us, event | category | flops | bytes accessed | tf_op | source)
XLA Modules:
  0.0 27.9 jit_solution(2595037751786402402)
XLA Ops:
  0.0 26.0 %shard_map.82 = bf16[1,16,16,1024]{3,2,1,0:T(8,128)(2,1)} custom-call(s32[128]{0:T(128)} %anchor.1, s32[128]{0:T(128)} %valid.1, bf16[16,16,1024]{2,1,0:T(8,128)(2,1)} %x_hbm.1, bf16[1,12,16,2048]{3,2,1,0:T(8,128)(2,1)} %bitcast.4, bf16[1,30,16,1024]{3,2,1,0:T(8,128)(2,1)} %bitcast.3, bf16[1,1024,3072]{2,1,0:T(8,128)(2,1)} %wqkv_hbm.1, ...), custom_call_target="tpu_custom_call" | custom-call | flops 2147483648 | bytes 12582912 | tf_op jit(solution)/shard_map/pallas_call | solution.py:517
  26.0 1.9 %copy.10 = bf16[1,16,16,1024]{3,2,1,0:T(8,128)(2,1)} copy(bf16[1,16,16,1024]{3,2,1,0:T(8,128)(2,1)} %shard_map.82) | data formatting | bytes 1048576

commit v4 on v3

--- a/solution.py
+++ b/solution.py
@@ -38,8 +38,7 @@
         pltpu.make_async_copy(wqkv_hbm.at[0], wqkv, load_sem.at[4]),
         pltpu.make_async_copy(wout_hbm.at[0], wout, load_sem.at[5]),
     ]
-    for load in loads:
-        load.start()
+    loads[0].start()
 
     barrier = pltpu.get_barrier_semaphore()
 
@@ -66,63 +65,25 @@
 
     lax.fori_loop(0, hosts, scan_send, 0, unroll=short)
     loads[0].wait()
-    pl.semaphore_wait(barrier, hosts)
-
-    def x_copy(to):
-        return pltpu.make_async_remote_copy(
-            src_ref=x_send.at[to], dst_ref=x_recv.at[me],
-            send_sem=xs_sem.at[to], recv_sem=xr_sem.at[me],
-            device_id={"stream": to}, device_id_type=MESH,
-        )
-
-    def x_arrival(source):
-        return pltpu.make_async_remote_copy(
-            src_ref=x_send.at[source], dst_ref=x_recv.at[source],
-            send_sem=xs_sem.at[source], recv_sem=xr_sem.at[source],
-            device_id={"stream": source}, device_id_type=MESH,
-        )
-
-    def y_copy(to):
-        return pltpu.make_async_remote_copy(
-            src_ref=y_send.at[to], dst_ref=y_recv.at[me],
-            send_sem=ys_sem.at[to], recv_sem=yr_sem.at[me],
-            device_id={"stream": to}, device_id_type=MESH,
-        )
-
-    def y_arrival(source):
-        return pltpu.make_async_remote_copy(
-            src_ref=y_send.at[source], dst_ref=y_recv.at[source],
-            send_sem=ys_sem.at[source], recv_sem=yr_sem.at[source],
-            device_id={"stream": source}, device_id_type=MESH,
-        )
-
-    def hand_over(chunk):
-        span = pl.ds(chunk * CHUNK, CHUNK)
-        return pltpu.make_async_remote_copy(
-            src_ref=y_work.at[span], dst_ref=x_work.at[span],
-            send_sem=hs_sem.at[chunk], recv_sem=hr_sem.at[chunk],
-            device_id={"section": 1 - section}, device_id_type=MESH,
-        )
-
-    @pl.when(section == 0)
-    def _():
-        def send(step, _):
+    for load in loads[1:]:
+        load.start()
+    @pl.when(section == 0)
+    def _():
+        def pack(step, _):
             to = lax.rem(me + step, hosts)
             x_send[to] = x_v[t_send[to]]
-            x_copy(to).start()
-            return 0
-
-        lax.fori_loop(1, hosts, send, 0)
+            return 0
+
+        lax.fori_loop(1, hosts, pack, 0)
 
     def scan_old(h, _):
-        found, count = jnp.int32(-1), jnp.int32(0)
+        found = jnp.int32(-1)
         for i in range(streams):
-            slot = anchor[h * streams + i]
-            hit = (lax.shift_right_arithmetic(slot, shift) == me) & (h != me)
-            found = jnp.where(hit, slot - base, found)
-            count = jnp.where(hit, valid[h * streams + i], count)
-        t_old[h] = found
-        t_count[h] = count
+            host = lax.shift_right_arithmetic(anchor[h * streams + i], shift)
+            found = jnp.where(host == me, i, found)
+        slot = h * streams + jnp.maximum(found, 0)
+        t_old[h] = jnp.where((found >= 0) & (h != me), anchor[slot] - base, -1)
+        t_count[h] = valid[slot]
         return 0
 
     lax.fori_loop(0, hosts, scan_old, 0, unroll=short)
@@ -151,10 +112,6 @@
             count = jnp.where(source == me, count, t_count[source])
         count_of[k] = count
 
-    loads[2].wait()
-    loads[1].wait()
-    loads[3].wait()
-
     span = ctx_rows * streams
     row = lax.broadcasted_iota(jnp.int32, (frames, span), 0)
     col = lax.broadcasted_iota(jnp.int32, (frames, span), 1)
@@ -163,20 +120,6 @@
         pick[pl.ds(k * frames, frames), :] = jnp.where(slant == perm[k], 1.0, 0.0).astype(
             jnp.bfloat16
         )
-
-    wide = 512
-
-    def place(i, _):
-        for part, to in enumerate((k_buf, v_buf)):
-            at = pl.multiple_of(i * wide, wide)
-            cached = ctx_v[:, :, pl.ds(part * width + at, wide)].reshape(span, wide)
-            cached = jnp.dot(pick[...], cached, preferred_element_type=jnp.float32)
-            cached = cached.astype(jnp.bfloat16)
-            for g in range(streams // group):
-                to[g, pl.ds(0, half), pl.ds(at, wide)] = cached[g * half : (g + 1) * half]
-        return 0
-
-    lax.fori_loop(0, width // wide, place, 0)
 
     steps = 10
     part_rows = steps * CHUNK
@@ -191,6 +134,83 @@
             blocks.append(jnp.where(col - t * streams == wanted, 1.0, 0.0))
     pick_kept[...] = jnp.concatenate(blocks, axis=0).astype(jnp.bfloat16)
 
+    row = lax.broadcasted_iota(jnp.int32, (2 * half, 2 * half), 0)
+    col = lax.broadcasted_iota(jnp.int32, (2 * half, 2 * half), 1)
+    col_stream = lax.shift_right_arithmetic(col, frames.bit_length() - 1) & (group - 1)
+    same = lax.shift_right_arithmetic(row, frames.bit_length() - 1) & (group - 1) == col_stream
+    col_frame = col & (frames - 1)
+    for g in range(streams // group):
+        limit = jnp.full((2 * half, 2 * half), ctx_rows, jnp.int32)
+        for i in range(group):
+            limit = jnp.where((col >= half) & (col_stream == i), count_of[g * group + i], limit)
+        bias[g] = jnp.where(same & (col_frame < limit), 0.0, -1e30)
+
+
+    pl.semaphore_wait(barrier, hosts)
+
+    def x_copy(to):
+        return pltpu.make_async_remote_copy(
+            src_ref=x_send.at[to], dst_ref=x_recv.at[me],
+            send_sem=xs_sem.at[to], recv_sem=xr_sem.at[me],
+            device_id={"stream": to}, device_id_type=MESH,
+        )
+
+    def x_arrival(source):
+        return pltpu.make_async_remote_copy(
+            src_ref=x_send.at[source], dst_ref=x_recv.at[source],
+            send_sem=xs_sem.at[source], recv_sem=xr_sem.at[source],
+            device_id={"stream": source}, device_id_type=MESH,
+        )
+
+    def y_copy(to):
+        return pltpu.make_async_remote_copy(
+            src_ref=y_send.at[to], dst_ref=y_recv.at[me],
+            send_sem=ys_sem.at[to], recv_sem=yr_sem.at[me],
+            device_id={"stream": to}, device_id_type=MESH,
+        )
+
+    def y_arrival(source):
+        return pltpu.make_async_remote_copy(
+            src_ref=y_send.at[source], dst_ref=y_recv.at[source],
+            send_sem=ys_sem.at[source], recv_sem=yr_sem.at[source],
+            device_id={"stream": source}, device_id_type=MESH,
+        )
+
+    def hand_over(chunk):
+        span = pl.ds(chunk * CHUNK, CHUNK)
+        return pltpu.make_async_remote_copy(
+            src_ref=y_work.at[span], dst_ref=x_work.at[span],
+            send_sem=hs_sem.at[chunk], recv_sem=hr_sem.at[chunk],
+            device_id={"section": 1 - section}, device_id_type=MESH,
+        )
+
+    @pl.when(section == 0)
+    def _():
+        def send(step, _):
+            to = lax.rem(me + step, hosts)
+            x_copy(to).start()
+            return 0
+
+        lax.fori_loop(1, hosts, send, 0)
+
+    loads[2].wait()
+    loads[1].wait()
+    loads[3].wait()
+
+    wide = 512
+
+    def place(i, _):
+        for part, to in enumerate((k_buf, v_buf)):
+            at = pl.multiple_of(i * wide, wide)
+            cached = ctx_v[:, :, pl.ds(part * width + at, wide)].reshape(span, wide)
+            cached = jnp.dot(pick[...], cached, preferred_element_type=jnp.float32)
+            cached = cached.astype(jnp.bfloat16)
+            for g in range(streams // group):
+                to[g, pl.ds(0, half), pl.ds(at, wide)] = cached[g * half : (g + 1) * half]
+        return 0
+
+    lax.fori_loop(0, width // wide, place, 0)
+
     def place_kept(i, _):
         at = pl.multiple_of(i * 2 * lanes, 2 * lanes)
         for b in range(kept_rows // steps):
@@ -205,18 +225,6 @@
         return 0
 
     lax.fori_loop(0, width // (2 * lanes), place_kept, 0)
-
-    row = lax.broadcasted_iota(jnp.int32, (2 * half, 2 * half), 0)
-    col = lax.broadcasted_iota(jnp.int32, (2 * half, 2 * half), 1)
-    col_stream = lax.shift_right_arithmetic(col, frames.bit_length() - 1) & (group - 1)
-    same = lax.shift_right_arithmetic(row, frames.bit_length() - 1) & (group - 1) == col_stream
-    col_frame = col & (frames - 1)
-    for g in range(streams // group):
-        limit = jnp.full((2 * half, 2 * half), ctx_rows, jnp.int32)
-        for i in range(group):
-            limit = jnp.where((col >= half) & (col_stream == i), count_of[g * group + i], limit)
-        bias[g] = jnp.where(same & (col_frame < limit), 0.0, -1e30)
-
 
     def conv_kept(chunk):
         def step(w, _):
@@ -421,7 +429,7 @@
 
     def assemble(i, _):
         source = lax.shift_right_arithmetic(anchor[base + i], shift)
-        out_ref[0, i] = jnp.where(source == me, y_work[rank[i]], y_recv[source])
+        out_ref[i] = jnp.where(source == me, y_work[rank[i]], y_recv[source])
         return 0
 
     lax.fori_loop(0, streams, assemble, 0)
@@ -441,6 +449,18 @@
         lax.fori_loop(1, hosts, x_sent, 0)
         hand_over(0).wait_send()
         hand_over(1).wait_send()
+
+
+def write_out(held, out_hbm, sem):
+    quarter = held.shape[0] // 4
+    copies = []
+    for i in range(4):
+        span = pl.ds(i * quarter, quarter)
+        copies.append(pltpu.make_async_copy(held.at[span], out_hbm.at[0, span], sem.at[i]))
+    for copy in copies:
+        copy.start()
+    for copy in copies:
+        copy.wait()
 
 
 def body(new_frames, valid, anchor, context, kept, wqkv, wout, wconv):
@@ -460,7 +480,7 @@
     dma = pltpu.SemaphoreType.DMA
     call = pl.pallas_call(
         functools.partial(kernel, hosts, streams, frames, width, ctx_rows, kept_rows, taps),
-        out_shape=jax.ShapeDtypeStruct((1, streams, frames, width), bf16),
+        out_shape=vmem((streams, frames, width), bf16),
         in_specs=[pl.BlockSpec(memory_space=pltpu.SMEM)] * 2
         + [pl.BlockSpec(memory_space=pl.ANY)] * 6,
         out_specs=pl.BlockSpec(memory_space=pltpu.VMEM),
@@ -514,7 +534,14 @@
             transcendentals=streams * frames * width,
         ),
     )
-    return call(anchor, valid, new_frames, context, kept, wqkv, wout, wconv)
+    held = call(anchor, valid, new_frames, context, kept, wqkv, wout, wconv)
+    return pl.pallas_call(
+        write_out,
+        out_shape=jax.ShapeDtypeStruct((1, streams, frames, width), bf16),
+        in_specs=[pl.BlockSpec(memory_space=pltpu.VMEM)],
+        out_specs=pl.BlockSpec(memory_space=pl.ANY),
+        scratch_shapes=[dma((4,))],
+    )(held)
 
 
 def solution(mesh):

time: 28 us -> 28.1 us (level)
  Pallas kernels: 26 us -> 27.1 us
  local copies, waits for them, and re-layouts: 1.88 us -> 0.78 us
    unnamed x1 -> x2, local copies, waits for them, and re-layouts: 1.88 us -> 0.78 us
    pallas_call x1 -> x2, Pallas kernels: 26 us -> 27.1 us  [the longest x1 25.2 us: body(): held = call(anchor, valid, new_frames, context, kept, wqkv, wout, wconv)]
where the time goes in v4:
time: 28.1 us; the launch traced here: 27.9 us
  Pallas kernels  27.1 us (96%)
  local copies, waits for them, and re-layouts  0.78 us (3%)
    pallas_call x1, Pallas kernels, body(): held = call(anchor, valid, new_frames, context, kept, wqkv, wout, wconv)  25.2 us
    pallas_call x1, Pallas kernels, body(): pl.pallas_call(write_out, out_shape=jax.ShapeDtypeStruct((1, streams, fra...  1.86 us
    unnamed x2, local copies, waits for them, and re-layouts  0.78 us

profile of v4, /device:TPU:1, one launch (start us, length us, event | category | flops | bytes accessed | tf_op | source)
XLA Modules:
  0.0 27.9 jit_solution(6319479654542558414)
XLA Ops:
  0.0 25.2 %shard_map.82.held = bf16[16,16,1024]{2,1,0:T(8,128)(2,1)S(1)} custom-call(s32[128]{0:T(128)} %anchor.1, s32[128]{0:T(128)} %valid.1, bf16[16,16,1024]{2,1,0:T(8,128)(2,1)} %x_hbm.1, bf16[1,12,16,2048]{3,2,1,0:T(8,128)(2,1)} %bitcast.4, bf16[1,30,16,1024]{3,2,1,0:T(8,128)(2,1)} %bitcast.3, bf16[1,1024,3072]{2,1,0:T(8,128)(2,1)} %wqkv_hbm.1, ...), custom_call_target="tpu_custom_call" | custom-call | flops 2147483648 | bytes 12582912 | tf_op jit(solution)/shard_map/pallas_call | solution.py:537
  25.2 0.0 copy-start
  25.2 0.8 %copy-done = bf16[16,16,1024]{2,1,0:T(8,128)(2,1)} copy-done((bf16[16,16,1024]{2,1,0:T(8,128)(2,1)}, bf16[16,16,1024]{2,1,0:T(8,128)(2,1)S(1)}, u32[]{:S(2)}) %copy-start) | copy-done | bytes 524312
  26.0 1.9 %shard_map.83 = bf16[1,16,16,1024]{3,2,1,0:T(8,128)(2,1)} custom-call(bf16[16,16,1024]{2,1,0:T(8,128)(2,1)} %copy-done), custom_call_target="tpu_custom_call" | custom-call | tf_op jit(solution)/shard_map/pallas_call | solution.py:538
Async XLA Ops:
  25.2 0.8 %copy-start = (bf16[16,16,1024]{2,1,0:T(8,128)(2,1)}, bf16[16,16,1024]{2,1,0:T(8,128)(2,1)S(1)}, u32[]{:S(2)}) copy-start(bf16[16,16,1024]{2,1,0:T(8,128)(2,1)S(1)} %shard_map.82.held) | copy-start | bytes 1572868

commit v5 on v4

v5 whole, which is shorter than its diff:
```python
import functools

import jax
import jax.numpy as jnp
from jax import lax
from jax.experimental import pallas as pl
from jax.experimental.pallas import tpu as pltpu
from jax.sharding import PartitionSpec as P

HEADS = 16
CHUNK = 4
BLOCK = 8
MESH = pl.DeviceIdType.MESH


def kernel(
    hosts, streams, frames, width, ctx_rows, kept_rows, taps,
    anchor, valid, x_hbm, ctx_hbm, kept_hbm, wqkv_hbm, wout_hbm, wconv_hbm, out_ref,
    x_v, ctx_v, kept_v, wqkv, wout, wconv, pick, pick_kept,
    x_send, x_recv, y_send, y_recv, x_work, y_work,
    normed, q_buf, k_buf, v_buf, att_buf, s_buf, p_buf, bias, res_buf, pad_t, conv_t, new_t, conv_o,
    t_send, t_old, t_count, rank, perm, host_of, count_of,
    load_sem, xs_sem, xr_sem, ys_sem, yr_sem, hs_sem, hr_sem,
):
    me = lax.axis_index("stream")
    section = lax.axis_index("section")
    base = me * streams
    rows = CHUNK * frames
    chunks = streams // CHUNK
    blocks = streams // BLOCK
    half = CHUNK * frames
    block_rows = BLOCK * frames
    lanes = 128

    loads = [
        pltpu.make_async_copy(x_hbm, x_v, load_sem.at[0]),
        pltpu.make_async_copy(kept_hbm.at[0], kept_v, load_sem.at[1]),
        pltpu.make_async_copy(ctx_hbm.at[0], ctx_v, load_sem.at[2]),
        pltpu.make_async_copy(wconv_hbm, wconv, load_sem.at[3]),
        pltpu.make_async_copy(wqkv_hbm.at[0], wqkv, load_sem.at[4]),
        pltpu.make_async_copy(wout_hbm.at[0], wout, load_sem.at[5]),
    ]
    loads[0].start()

    barrier = pltpu.get_barrier_semaphore()

    def greet(step, _):
        pl.semaphore_signal(
            barrier, inc=1, device_id={"stream": lax.rem(me + step, hosts)}, device_id_type=MESH
        )
        return 0

    lax.fori_loop(1, hosts, greet, 0)
    pl.semaphore_signal(barrier, inc=1, device_id={"section": 1 - section}, device_id_type=MESH)

    shift = streams.bit_length() - 1
    own = [anchor[base + i] for i in range(streams)]
    own_host = [lax.shift_right_arithmetic(a, shift) for a in own]
    short = hosts <= 8

    def scan_send(h, _):
        found = jnp.int32(0)
        for i in range(streams):
            found = jnp.where(own_host[i] == h, i, found)
        t_send[h] = found
        return 0

    lax.fori_loop(0, hosts, scan_send, 0, unroll=short)
    loads[0].wait()
    for load in loads[1:]:
        load.start()
    @pl.when(section == 0)
    def _():
        def pack(step, _):
            to = lax.rem(me + step, hosts)
            x_send[to] = x_v[t_send[to]]
            return 0

        lax.fori_loop(1, hosts, pack, 0)

    def scan_old(h, _):
        found = jnp.int32(-1)
        for i in range(streams):
            host = lax.shift_right_arithmetic(anchor[h * streams + i], shift)
            found = jnp.where(host == me, i, found)
        slot = h * streams + jnp.maximum(found, 0)
        t_old[h] = jnp.where((found >= 0) & (h != me), anchor[slot] - base, -1)
        t_count[h] = valid[slot]
        return 0

    lax.fori_loop(0, hosts, scan_old, 0, unroll=short)
    stays = [(h == me).astype(jnp.int32) for h in own_host]
    moved = streams - sum(stays)
    gone, left = jnp.int32(CHUNK), jnp.int32(0)
    ranks = []
    for i in range(streams):
        place_left = jnp.where(left < CHUNK, left, left + moved)
        ranks.append(jnp.minimum(jnp.where(own_host[i] == me, place_left, gone), streams - 1))
        rank[i] = ranks[i]
        left = left + stays[i]
        gone = gone + 1 - stays[i]
    for k in range(streams):
        old = jnp.int32(0)
        for i in range(streams):
            old = jnp.where(ranks[i] == k, i, old)
        perm[k] = old
        count = valid[base + old]
        if CHUNK <= k < CHUNK + BLOCK:

            def scan_host(h, found):
                return jnp.where(t_old[h] == old, h, found)

            source = lax.fori_loop(0, hosts, scan_host, me, unroll=short)
            host_of[k] = source
            count = jnp.where(source == me, count, t_count[source])
        count_of[k] = count

    span = ctx_rows * streams
    row = lax.broadcasted_iota(jnp.int32, (frames, span), 0)
    col = lax.broadcasted_iota(jnp.int32, (frames, span), 1)
    slant = col - row * streams
    for k in range(streams):
        pick[pl.ds(k * frames, frames), :] = jnp.where(slant == perm[k], 1.0, 0.0).astype(
            jnp.bfloat16
        )

    steps = 10
    part_rows = steps * BLOCK
    sub = lax.broadcasted_iota(jnp.int32, (BLOCK, steps * streams), 0)
    col = lax.broadcasted_iota(jnp.int32, (BLOCK, steps * streams), 1)
    picks = []
    for block in range(blocks):
        wanted = jnp.zeros((BLOCK, steps * streams), jnp.int32)
        for i in range(BLOCK):
            wanted = jnp.where(sub == i, perm[block * BLOCK + i], wanted)
        for t in range(steps):
            picks.append(jnp.where(col - t * streams == wanted, 1.0, 0.0))
    pick_kept[...] = jnp.concatenate(picks, axis=0).astype(jnp.bfloat16)

    row = lax.broadcasted_iota(jnp.int32, (2 * half, 2 * half), 0)
    col = lax.broadcasted_iota(jnp.int32, (2 * half, 2 * half), 1)
    col_stream = lax.shift_right_arithmetic(col, frames.bit_length() - 1) & (CHUNK - 1)
    same = lax.shift_right_arithmetic(row, frames.bit_length() - 1) & (CHUNK - 1) == col_stream
    col_frame = col & (frames - 1)
    for g in range(chunks):
        limit = jnp.full((2 * half, 2 * half), ctx_rows, jnp.int32)
        for i in range(CHUNK):
            limit = jnp.where((col >= half) & (col_stream == i), count_of[g * CHUNK + i], limit)
        bias[g] = jnp.where(same & (col_frame < limit), 0.0, -1e30)


    pl.semaphore_wait(barrier, hosts)

    def x_copy(to):
        return pltpu.make_async_remote_copy(
            src_ref=x_send.at[to], dst_ref=x_recv.at[me],
            send_sem=xs_sem.at[to], recv_sem=xr_sem.at[me],
            device_id={"stream": to}, device_id_type=MESH,
        )

    def x_arrival(source):
        return pltpu.make_async_remote_copy(
            src_ref=x_send.at[source], dst_ref=x_recv.at[source],
            send_sem=xs_sem.at[source], recv_sem=xr_sem.at[source],
            device_id={"stream": source}, device_id_type=MESH,
        )

    def y_copy(to):
        return pltpu.make_async_remote_copy(
            src_ref=y_send.at[to], dst_ref=y_recv.at[me],
            send_sem=ys_sem.at[to], recv_sem=yr_sem.at[me],
            device_id={"stream": to}, device_id_type=MESH,
        )

    def y_arrival(source):
        return pltpu.make_async_remote_copy(
            src_ref=y_send.at[source], dst_ref=y_recv.at[source],
            send_sem=ys_sem.at[source], recv_sem=yr_sem.at[source],
            device_id={"stream": source}, device_id_type=MESH,
        )

    def hand_over(chunk):
        span = pl.ds(chunk * CHUNK, CHUNK)
        return pltpu.make_async_remote_copy(
            src_ref=y_work.at[span], dst_ref=x_work.at[span],
            send_sem=hs_sem.at[chunk], recv_sem=hr_sem.at[chunk],
            device_id={"section": 1 - section}, device_id_type=MESH,
        )

    @pl.when(section == 0)
    def _():
        def send(step, _):
            to = lax.rem(me + step, hosts)
            x_copy(to).start()
            return 0

        lax.fori_loop(1, hosts, send, 0)

    loads[2].wait()
    loads[1].wait()
    loads[3].wait()

    wide = 512

    def place(i, _):
        for part, to in enumerate((k_buf, v_buf)):
            at = pl.multiple_of(i * wide, wide)
            cached = ctx_v[:, :, pl.ds(part * width + at, wide)].reshape(span, wide)
            cached = jnp.dot(pick[...], cached, preferred_element_type=jnp.float32)
            cached = cached.astype(jnp.bfloat16)
            for g in range(chunks):
                to[g, pl.ds(0, half), pl.ds(at, wide)] = cached[g * half : (g + 1) * half]
        return 0

    lax.fori_loop(0, width // wide, place, 0)

    def place_kept(i, _):
        at = pl.multiple_of(i * 2 * lanes, 2 * lanes)
        for b in range(kept_rows // steps):
            kept = kept_v[pl.ds(b * steps, steps), :, pl.ds(at, 2 * lanes)]
            kept = kept.reshape(steps * streams, 2 * lanes)
            kept = jnp.dot(pick_kept[...], kept, preferred_element_type=jnp.float32)
            for block in range(blocks):
                for w in range(2):
                    pad_t[block, 2 * i + w, pl.ds(b * part_rows, part_rows), :] = kept[
                        block * part_rows : (block + 1) * part_rows, w * lanes : (w + 1) * lanes
                    ]
        return 0

    lax.fori_loop(0, width // (2 * lanes), place_kept, 0)

    def conv_kept(block):
        def step(w, _):
            at = pl.ds(pl.multiple_of(w * lanes, lanes), lanes)
            total = jnp.zeros((block_rows, lanes), jnp.float32)
            for j in range(kept_rows):
                n = min(frames, kept_rows - j) * BLOCK
                term = wconv[j, :, at] * pad_t[block, w, pl.ds(j * BLOCK, n), :]
                if n < block_rows:
                    total = jnp.concatenate([total[:n] + term, total[n:]], axis=0)
                else:
                    total = total + term
            conv_t[block, w] = total
            return 0

        lax.fori_loop(0, width // lanes, step, 0)

    conv_kept(0)

    def project(chunk):
        x = x_work[pl.ds(chunk * CHUNK, CHUNK)].reshape(half, width).astype(jnp.float32)
        centred = x - jnp.mean(x, axis=-1, keepdims=True)
        variance = jnp.mean(centred * centred, axis=-1, keepdims=True)
        normed[...] = (centred * lax.rsqrt(variance + 1e-05)).astype(jnp.bfloat16)
        for part, to in enumerate((q_buf, k_buf, v_buf)):
            got = jnp.dot(
                normed[...], wqkv[:, part * width : (part + 1) * width],
                preferred_element_type=jnp.float32,
            )
            if part == 0:
                to[...] = (got * (width // HEADS) ** (-0.5)).astype(jnp.bfloat16)
            else:
                to[chunk, half:, :] = got.astype(jnp.bfloat16)

    def finish(chunk):
        lane = lax.broadcasted_iota(jnp.int32, (half, lanes), 1)
        first = lane < lanes // 2
        mask = bias[chunk]
        pairs = [pl.ds(p * lanes, lanes) for p in range(width // lanes)]
        for p, at in enumerate(pairs):
            q = q_buf[:, at]
            none = jnp.zeros_like(q)
            q = jnp.concatenate([jnp.where(first, q, none), jnp.where(first, none, q)], axis=0)
            s_buf[p] = lax.dot_general(
                q, k_buf[chunk, :, at], (((1,), (1,)), ((), ())),
                preferred_element_type=jnp.float32,
            )
        for p, at in enumerate(pairs):
            scores = s_buf[p] + mask
            p_buf[p] = jnp.exp(scores - jnp.max(scores, axis=-1, keepdims=True)).astype(
                jnp.bfloat16
            )
        ones = jnp.ones((2 * half, lanes), jnp.bfloat16)
        for p, at in enumerate(pairs):
            values = jnp.concatenate([v_buf[chunk, :, at], ones], axis=1)
            mixed = jnp.dot(p_buf[p], values, preferred_element_type=jnp.float32)
            top = jnp.where(first, mixed[:half, :lanes], mixed[half:, :lanes])
            total = jnp.where(first, mixed[:half, lanes:], mixed[half:, lanes:])
            att_buf[:, at] = (top / total).astype(jnp.bfloat16)

        got = jnp.dot(att_buf[...], wout[...], preferred_element_type=jnp.float32)
        x = x_work[pl.ds(chunk * CHUNK, CHUNK)].reshape(half, width).astype(jnp.float32)
        res_buf[...] = x + got

        block = lax.shift_right_arithmetic(chunk, 1)
        offset = (chunk & 1) * CHUNK
        for s in range(CHUNK):
            own = res_buf[s * frames : (s + 1) * frames, :]
            own = own.astype(jnp.bfloat16).astype(jnp.float32)
            for w in range(width // lanes):
                new_t[w, pl.ds(offset + s, frames, stride=BLOCK), :] = own[
                    :, w * lanes : (w + 1) * lanes
                ]

        def conv_new(w, _):
            at = pl.ds(pl.multiple_of(w * lanes, lanes), lanes)
            total = conv_t[block, w]
            for j in range(taps - frames, taps):
                start = (kept_rows - j) * BLOCK
                term = wconv[j, :, at] * new_t[w, pl.ds(0, block_rows - start), :]
                if start:
                    total = jnp.concatenate([total[:start], total[start:] + term], axis=0)
                else:
                    total = total + term
            conv_o[w] = total / (1.0 + jnp.exp(-total))
            return 0

        lax.fori_loop(0, width // lanes, conv_new, 0, unroll=2)

        frame = lax.broadcasted_iota(jnp.int32, (frames, width), 0)
        for s in range(CHUNK):
            k = chunk * CHUNK + s
            own = res_buf[s * frames : (s + 1) * frames, :]
            own = own + jnp.concatenate(
                [
                    conv_o[w, pl.ds(offset + s, frames, stride=BLOCK), :]
                    for w in range(width // lanes)
                ],
                axis=1,
            )
            y_work[k] = jnp.where(frame < count_of[k], own, 0.0).astype(jnp.bfloat16)

    def give_back(step, _):
        to = lax.rem(me + step, hosts)
        y_send[to] = y_work[rank[jnp.maximum(t_old[to], 0)]]
        y_copy(to).start()
        return 0

    @pl.when(section == 0)
    def _():
        for k in range(CHUNK):
            x_work[k] = x_v[perm[k]]

    @pl.when(section == 1)
    def _():
        conv_kept(1)

    loads[4].wait()
    loads[5].wait()

    def turn(chunk, _):
        @pl.when((section == 0) & (chunk == 1))
        def _():
            conv_kept(1)

            def arrive(step, _):
                x_arrival(lax.rem(me + step, hosts)).wait_recv()
                return 0

            lax.fori_loop(1, hosts, arrive, 0)

            def fill(k, _):
                x_work[k] = x_v[perm[k]]
                return 0

            def fill_moved(k, _):
                source = host_of[k]
                x_work[k] = jnp.where(source == me, x_v[perm[k]], x_recv[source])
                return 0

            lax.fori_loop(CHUNK, CHUNK + BLOCK, fill_moved, 0)
            lax.fori_loop(CHUNK + BLOCK, streams, fill, 0)

        @pl.when(section == 1)
        def _():
            hand_over(chunk).wait_recv()

        project(chunk)
        finish(chunk)

        @pl.when(section == 0)
        def _():
            hand_over(chunk).start()

        @pl.when(chunk == BLOCK // CHUNK)
        def _():
            lax.fori_loop(1, hosts, give_back, 0)

        return 0

    lax.fori_loop(0, chunks, turn, 0)

    def returned(step, _):
        y_arrival(lax.rem(me + step, hosts)).wait_recv()
        return 0

    lax.fori_loop(1, hosts, returned, 0)

    def assemble(i, _):
        source = lax.shift_right_arithmetic(anchor[base + i], shift)
        out_ref[i] = jnp.where(source == me, y_work[rank[i]], y_recv[source])
        return 0

    lax.fori_loop(0, streams, assemble, 0)

    def sent(step, _):
        y_copy(lax.rem(me + step, hosts)).wait_send()
        return 0

    lax.fori_loop(1, hosts, sent, 0)

    @pl.when(section == 0)
    def _():
        def x_sent(step, _):
            x_copy(lax.rem(me + step, hosts)).wait_send()
            return 0

        lax.fori_loop(1, hosts, x_sent, 0)
        for chunk in range(chunks):
            hand_over(chunk).wait_send()


def body(new_frames, valid, anchor, context, kept, wqkv, wout, wconv):
    streams, frames, width = new_frames.shape
    hosts = lax.axis_size("stream")
    ctx_rows, kept_rows, taps = context.shape[2], kept.shape[2], wconv.shape[1]
    context = jnp.transpose(context, (0, 2, 1, 3))
    kept = jnp.transpose(kept, (0, 2, 1, 3))
    wconv = jnp.transpose(wconv, (1, 0, 2))
    assert streams == 2 * BLOCK and BLOCK == 2 * CHUNK and lax.axis_size("section") == 2
    assert frames == 16 and taps == kept_rows + 1 and kept_rows % 10 == 0
    assert streams & (streams - 1) == 0
    chunks, blocks, tiles = streams // CHUNK, streams // BLOCK, width // 128
    rows = CHUNK * frames
    bf16, f32, i32 = jnp.bfloat16, jnp.float32, jnp.int32
    vmem, smem = pltpu.VMEM, pltpu.SMEM
    dma = pltpu.SemaphoreType.DMA
    call = pl.pallas_call(
        functools.partial(kernel, hosts, streams, frames, width, ctx_rows, kept_rows, taps),
        out_shape=vmem((streams, frames, width), bf16),
        in_specs=[pl.BlockSpec(memory_space=pltpu.SMEM)] * 2
        + [pl.BlockSpec(memory_space=pl.ANY)] * 6,
        out_specs=pl.BlockSpec(memory_space=pltpu.VMEM),
        scratch_shapes=[
            vmem((streams, frames, width), bf16),
            vmem((ctx_rows, streams, 2 * width), bf16),
            vmem((kept_rows, streams, width), bf16),
            vmem((width, 3 * width), bf16),
            vmem((width, width), bf16),
            vmem((taps, 1, width), f32),
            vmem((streams * frames, ctx_rows * streams), bf16),
            vmem((10 * streams, 10 * streams), bf16),
            vmem((hosts, frames, width), bf16),
            vmem((hosts, frames, width), bf16),
            vmem((hosts, frames, width), bf16),
            vmem((hosts, frames, width), bf16),
            vmem((streams, frames, width), bf16),
            vmem((streams, frames, width), bf16),
            vmem((rows, width), bf16),
            vmem((rows, width), bf16),
            vmem((chunks, 2 * rows, width), bf16),
            vmem((chunks, 2 * rows, width), bf16),
            vmem((rows, width), bf16),
            vmem((tiles, 2 * rows, 2 * rows), f32),
            vmem((tiles, 2 * rows, 2 * rows), bf16),
            vmem((chunks, 2 * rows, 2 * rows), f32),
            vmem((rows, width), f32),
            vmem((blocks, tiles, kept_rows * BLOCK, 128), f32),
            vmem((blocks, tiles, frames * BLOCK, 128), f32),
            vmem((tiles, frames * BLOCK, 128), f32),
            vmem((tiles, frames * BLOCK, 128), f32),
            smem((hosts,), i32),
            smem((hosts,), i32),
            smem((hosts,), i32),
            smem((streams,), i32),
            smem((streams,), i32),
            smem((streams,), i32),
            smem((streams,), i32),
            dma((6,)),
            dma((hosts,)),
            dma((hosts,)),
            dma((hosts,)),
            dma((hosts,)),
            dma((chunks,)),
            dma((chunks,)),
        ],
        compiler_params=pltpu.CompilerParams(
            collective_id=0, has_side_effects=True, vmem_limit_bytes=56 * 1024 * 1024
        ),
        cost_estimate=pl.CostEstimate(
            flops=2 * streams * frames * width * width * 4,
            bytes_accessed=12 * 1024 * 1024,
            transcendentals=streams * frames * width,
        ),
    )
    held = call(anchor, valid, new_frames, context, kept, wqkv, wout, wconv)
    return held[None]


def solution(mesh):
    return jax.shard_map(
        body,
        mesh=mesh,
        in_specs=(
            P(("groups", "stream"), None, None),
            P("groups"),
            P("groups"),
            P("section", ("groups", "stream"), None, None),
            P("section", ("groups", "stream"), None, None),
            P("section", None, None),
            P("section", None, None),
            P("section", None, None),
        ),
        out_specs=P("section", ("groups", "stream"), None, None),
        check_vma=False,
    )
```

time: 28.1 us -> 27.8 us (0.989)
  Pallas kernels: 27.1 us -> 26.8 us
    pallas_call x1 -> x0, Pallas kernels: 1.86 us -> none  [body(): pl.pallas_call(write_out, out_shape=jax.ShapeDtypeStruct((1, streams, fra...]
    pallas_call x1, Pallas kernels: 25.2 us -> 26.8 us  [body(): held = call(anchor, valid, new_frames, context, kept, wqkv, wout, wconv)]
    unnamed x2 -> x1, local copies, waits for them, and re-layouts: 0.78 us -> 0.8 us
where the time goes in v5:
time: 27.8 us; the launch traced here: 27.6 us
  Pallas kernels  26.8 us (96%)
  local copies, waits for them, and re-layouts  0.8 us (3%)
    pallas_call x1, Pallas kernels, body(): held = call(anchor, valid, new_frames, context, kept, wqkv, wout, wconv)  26.8 us
    unnamed x1, local copies, waits for them, and re-layouts  0.8 us

profile of v5, /device:TPU:1, one launch (start us, length us, event | category | flops | bytes accessed | tf_op | source)
XLA Modules:
  0.0 27.6 jit_solution(6054687493683934025)
XLA Ops:
  0.0 26.8 %shard_map.82 = bf16[16,16,1024]{2,1,0:T(8,128)(2,1)S(1)} custom-call(s32[128]{0:T(128)} %anchor.1, s32[128]{0:T(128)} %valid.1, bf16[16,16,1024]{2,1,0:T(8,128)(2,1)} %x_hbm.1, bf16[1,12,16,2048]{3,2,1,0:T(8,128)(2,1)} %bitcast.6, bf16[1,30,16,1024]{3,2,1,0:T(8,128)(2,1)} %bitcast.5, bf16[1,1024,3072]{2,1,0:T(8,128)(2,1)} %wqkv_hbm.1, ...), custom_call_target="tpu_custom_call" | custom-call | flops 2147483648 | bytes 12582912 | tf_op jit(solution)/shard_map/pallas_call | solution.py:496
  26.8 0.8 %copy.10 = bf16[1,16,16,1024]{3,2,1,0:T(8,128)(2,1)} copy(bf16[1,16,16,1024]{3,2,1,0:T(8,128)(2,1)S(1)} %bitcast.4) | data formatting | bytes 1048576

commit v6 on v5

--- a/solution.py
+++ b/solution.py
@@ -10,6 +10,7 @@
 HEADS = 16
 CHUNK = 4
 BLOCK = 8
+LOADS = 25
 MESH = pl.DeviceIdType.MESH
 
 
@@ -32,15 +33,34 @@
     block_rows = BLOCK * frames
     lanes = 128
 
-    loads = [
-        pltpu.make_async_copy(x_hbm, x_v, load_sem.at[0]),
-        pltpu.make_async_copy(kept_hbm.at[0], kept_v, load_sem.at[1]),
-        pltpu.make_async_copy(ctx_hbm.at[0], ctx_v, load_sem.at[2]),
-        pltpu.make_async_copy(wconv_hbm, wconv, load_sem.at[3]),
-        pltpu.make_async_copy(wqkv_hbm.at[0], wqkv, load_sem.at[4]),
-        pltpu.make_async_copy(wout_hbm.at[0], wout, load_sem.at[5]),
-    ]
-    loads[0].start()
+    slots = iter(range(LOADS))
+
+    def load(source, target):
+        copy = pltpu.make_async_copy(source, target, load_sem.at[next(slots)])
+        copy.start()
+        return copy
+
+    def load_blocks(source, target, count):
+        size = target.shape[0] // count
+        spans = [pl.ds(i * size, size) for i in range(count)]
+        return [load(source.at[span], target.at[span]) for span in spans]
+
+    def load_weight(source, target, part):
+        at = pl.ds(part * width, width)
+        return load_blocks(source.at[:, at], target.at[:, at], 4)
+
+    def wait_for(copies):
+        for copy in copies:
+            copy.wait()
+
+    x_loads = load_blocks(x_hbm, x_v, 2)
+    kept_loads = load_blocks(kept_hbm.at[0], kept_v, 3)
+    ctx_loads = load_blocks(ctx_hbm.at[0], ctx_v, 3)
+    conv_loads = [load(wconv_hbm, wconv)]
+    qkv_loads = []
+    for part in range(3):
+        qkv_loads += load_weight(wqkv_hbm.at[0], wqkv, part)
+    out_loads = load_weight(wout_hbm.at[0], wout, 0)
 
     barrier = pltpu.get_barrier_semaphore()
 
@@ -66,9 +86,7 @@
         return 0
 
     lax.fori_loop(0, hosts, scan_send, 0, unroll=short)
-    loads[0].wait()
-    for load in loads[1:]:
-        load.start()
+    wait_for(x_loads)
     @pl.when(section == 0)
     def _():
         def pack(step, _):
@@ -196,9 +214,7 @@
 
         lax.fori_loop(1, hosts, send, 0)
 
-    loads[2].wait()
-    loads[1].wait()
-    loads[3].wait()
+    wait_for(ctx_loads + kept_loads + conv_loads)
 
     wide = 512
 
@@ -345,8 +361,7 @@
     def _():
         conv_kept(1)
 
-    loads[4].wait()
-    loads[5].wait()
+    wait_for(qkv_loads)
 
     def turn(chunk, _):
         @pl.when((section == 0) & (chunk == 1))
@@ -376,6 +391,11 @@
             hand_over(chunk).wait_recv()
 
         project(chunk)
+
+        @pl.when(chunk == 0)
+        def _():
+            wait_for(out_loads)
+
         finish(chunk)
 
         @pl.when(section == 0)
@@ -476,7 +496,7 @@
             smem((streams,), i32),
             smem((streams,), i32),
             smem((streams,), i32),
-            dma((6,)),
+            dma((LOADS,)),
             dma((hosts,)),
             dma((hosts,)),
             dma((hosts,)),

time: 27.8 us -> 27.9 us (level)
  no operation moved by 1% of the time
where the time goes in v6:
time: 27.9 us; the launch traced here: 27.7 us
  Pallas kernels  26.9 us (96%)
  local copies, waits for them, and re-layouts  0.8 us (3%)
    pallas_call x1, Pallas kernels, body(): held = call(anchor, valid, new_frames, context, kept, wqkv, wout, wconv)  26.9 us
    unnamed x1, local copies, waits for them, and re-layouts  0.8 us

profile of v6, /device:TPU:1, one launch (start us, length us, event | category | flops | bytes accessed | tf_op | source)
XLA Modules:
  0.0 27.7 jit_solution(190518516075277499)
XLA Ops:
  0.0 26.9 %shard_map.82 = bf16[16,16,1024]{2,1,0:T(8,128)(2,1)S(1)} custom-call(s32[128]{0:T(128)} %anchor.1, s32[128]{0:T(128)} %valid.1, bf16[16,16,1024]{2,1,0:T(8,128)(2,1)} %x_hbm.1, bf16[1,12,16,2048]{3,2,1,0:T(8,128)(2,1)} %bitcast.6, bf16[1,30,16,1024]{3,2,1,0:T(8,128)(2,1)} %bitcast.5, bf16[1,1024,3072]{2,1,0:T(8,128)(2,1)} %wqkv_hbm.1, ...), custom_call_target="tpu_custom_call" | custom-call | flops 2147483648 | bytes 12582912 | tf_op jit(solution)/shard_map/pallas_call | solution.py:516
  26.9 0.8 %copy.10 = bf16[1,16,16,1024]{3,2,1,0:T(8,128)(2,1)} copy(bf16[1,16,16,1024]{3,2,1,0:T(8,128)(2,1)S(1)} %bitcast.4) | data formatting | bytes 1048576

commit v7 on v6

--- a/solution.py
+++ b/solution.py
@@ -86,16 +86,6 @@
         return 0
 
     lax.fori_loop(0, hosts, scan_send, 0, unroll=short)
-    wait_for(x_loads)
-    @pl.when(section == 0)
-    def _():
-        def pack(step, _):
-            to = lax.rem(me + step, hosts)
-            x_send[to] = x_v[t_send[to]]
-            return 0
-
-        lax.fori_loop(1, hosts, pack, 0)
-
     def scan_old(h, _):
         found = jnp.int32(-1)
         for i in range(streams):
@@ -133,6 +123,63 @@
             count = jnp.where(source == me, count, t_count[source])
         count_of[k] = count
 
+    wait_for(x_loads)
+    @pl.when(section == 0)
+    def _():
+        def pack(step, _):
+            to = lax.rem(me + step, hosts)
+            x_send[to] = x_v[t_send[to]]
+            return 0
+
+        lax.fori_loop(1, hosts, pack, 0)
+
+    pl.semaphore_wait(barrier, hosts)
+
+    def x_copy(to):
+        return pltpu.make_async_remote_copy(
+            src_ref=x_send.at[to], dst_ref=x_recv.at[me],
+            send_sem=xs_sem.at[to], recv_sem=xr_sem.at[me],
+            device_id={"stream": to}, device_id_type=MESH,
+        )
+
+    def x_arrival(source):
+        return pltpu.make_async_remote_copy(
+            src_ref=x_send.at[source], dst_ref=x_recv.at[source],
+            send_sem=xs_sem.at[source], recv_sem=xr_sem.at[source],
+            device_id={"stream": source}, device_id_type=MESH,
+        )
+
+    def y_copy(to):
+        return pltpu.make_async_remote_copy(
+            src_ref=y_send.at[to], dst_ref=y_recv.at[me],
+            send_sem=ys_sem.at[to], recv_sem=yr_sem.at[me],
+            device_id={"stream": to}, device_id_type=MESH,
+        )
+
+    def y_arrival(source):
+        return pltpu.make_async_remote_copy(
+            src_ref=y_send.at[source], dst_ref=y_recv.at[source],
+            send_sem=ys_sem.at[source], recv_sem=yr_sem.at[source],
+            device_id={"stream": source}, device_id_type=MESH,
+        )
+
+    def hand_over(chunk):
+        span = pl.ds(chunk * CHUNK, CHUNK)
+        return pltpu.make_async_remote_copy(
+            src_ref=y_work.at[span], dst_ref=x_work.at[span],
+            send_sem=hs_sem.at[chunk], recv_sem=hr_sem.at[chunk],
+            device_id={"section": 1 - section}, device_id_type=MESH,
+        )
+
+    @pl.when(section == 0)
+    def _():
+        def send(step, _):
+            to = lax.rem(me + step, hosts)
+            x_copy(to).start()
+            return 0
+
+        lax.fori_loop(1, hosts, send, 0)
+
     span = ctx_rows * streams
     row = lax.broadcasted_iota(jnp.int32, (frames, span), 0)
     col = lax.broadcasted_iota(jnp.int32, (frames, span), 1)
@@ -167,53 +214,6 @@
         bias[g] = jnp.where(same & (col_frame < limit), 0.0, -1e30)
 
 
-    pl.semaphore_wait(barrier, hosts)
-
-    def x_copy(to):
-        return pltpu.make_async_remote_copy(
-            src_ref=x_send.at[to], dst_ref=x_recv.at[me],
-            send_sem=xs_sem.at[to], recv_sem=xr_sem.at[me],
-            device_id={"stream": to}, device_id_type=MESH,
-        )
-
-    def x_arrival(source):
-        return pltpu.make_async_remote_copy(
-            src_ref=x_send.at[source], dst_ref=x_recv.at[source],
-            send_sem=xs_sem.at[source], recv_sem=xr_sem.at[source],
-            device_id={"stream": source}, device_id_type=MESH,
-        )
-
-    def y_copy(to):
-        return pltpu.make_async_remote_copy(
-            src_ref=y_send.at[to], dst_ref=y_recv.at[me],
-            send_sem=ys_sem.at[to], recv_sem=yr_sem.at[me],
-            device_id={"stream": to}, device_id_type=MESH,
-        )
-
-    def y_arrival(source):
-        return pltpu.make_async_remote_copy(
-            src_ref=y_send.at[source], dst_ref=y_recv.at[source],
-            send_sem=ys_sem.at[source], recv_sem=yr_sem.at[source],
-            device_id={"stream": source}, device_id_type=MESH,
-        )
-
-    def hand_over(chunk):
-        span = pl.ds(chunk * CHUNK, CHUNK)
-        return pltpu.make_async_remote_copy(
-            src_ref=y_work.at[span], dst_ref=x_work.at[span],
-            send_sem=hs_sem.at[chunk], recv_sem=hr_sem.at[chunk],
-            device_id={"section": 1 - section}, device_id_type=MESH,
-        )
-
-    @pl.when(section == 0)
-    def _():
-        def send(step, _):
-            to = lax.rem(me + step, hosts)
-            x_copy(to).start()
-            return 0
-
-        lax.fori_loop(1, hosts, send, 0)
-
     wait_for(ctx_loads + kept_loads + conv_loads)
 
     wide = 512
@@ -248,15 +248,15 @@
     def conv_kept(block):
         def step(w, _):
             at = pl.ds(pl.multiple_of(w * lanes, lanes), lanes)
-            total = jnp.zeros((block_rows, lanes), jnp.float32)
+            window = [pad_t[block, w, t * BLOCK : (t + 1) * BLOCK, :] for t in range(kept_rows)]
+            totals = [None] * frames
             for j in range(kept_rows):
-                n = min(frames, kept_rows - j) * BLOCK
-                term = wconv[j, :, at] * pad_t[block, w, pl.ds(j * BLOCK, n), :]
-                if n < block_rows:
-                    total = jnp.concatenate([total[:n] + term, total[n:]], axis=0)
-                else:
-                    total = total + term
-            conv_t[block, w] = total
+                tap = jnp.broadcast_to(wconv[j, :, at], (BLOCK, lanes))
+                for t in range(min(frames, kept_rows - j)):
+                    term = tap * window[t + j]
+                    totals[t] = term if j == 0 else totals[t] + term
+            for t in range(frames):
+                conv_t[block, w, t * BLOCK : (t + 1) * BLOCK, :] = totals[t]
             return 0
 
         lax.fori_loop(0, width // lanes, step, 0)
@@ -320,18 +320,19 @@
 
         def conv_new(w, _):
             at = pl.ds(pl.multiple_of(w * lanes, lanes), lanes)
-            total = conv_t[block, w]
+            window = [new_t[w, t * BLOCK : (t + 1) * BLOCK, :] for t in range(frames)]
+            totals = [conv_t[block, w, t * BLOCK : (t + 1) * BLOCK, :] for t in range(frames)]
             for j in range(taps - frames, taps):
-                start = (kept_rows - j) * BLOCK
-                term = wconv[j, :, at] * new_t[w, pl.ds(0, block_rows - start), :]
-                if start:
-                    total = jnp.concatenate([total[:start], total[start:] + term], axis=0)
-                else:
-                    total = total + term
-            conv_o[w] = total / (1.0 + jnp.exp(-total))
+                tap = jnp.broadcast_to(wconv[j, :, at], (BLOCK, lanes))
+                first_t = kept_rows - j
+                for t in range(first_t, frames):
+                    totals[t] = totals[t] + tap * window[t - first_t]
+            for t in range(frames):
+                part = 0.5 * totals[t]
+                conv_o[w, t * BLOCK : (t + 1) * BLOCK, :] = part + part * jnp.tanh(part)
             return 0
 
-        lax.fori_loop(0, width // lanes, conv_new, 0, unroll=2)
+        lax.fori_loop(0, width // lanes, conv_new, 0)
 
         frame = lax.broadcasted_iota(jnp.int32, (frames, width), 0)
         for s in range(CHUNK):

time: 27.9 us -> 28 us (level)
  no operation moved by 1% of the time
where the time goes in v7:
time: 28 us; the launch traced here: 27.8 us
  Pallas kernels  27 us (96%)
  local copies, waits for them, and re-layouts  0.8 us (3%)
    pallas_call x1, Pallas kernels, body(): held = call(anchor, valid, new_frames, context, kept, wqkv, wout, wconv)  27 us
    unnamed x1, local copies, waits for them, and re-layouts  0.8 us

profile of v7, /device:TPU:1, one launch (start us, length us, event | category | flops | bytes accessed | tf_op | source)
XLA Modules:
  0.0 27.8 jit_solution(16140073779091252305)
XLA Ops:
  0.0 27.0 %shard_map.82 = bf16[16,16,1024]{2,1,0:T(8,128)(2,1)S(1)} custom-call(s32[128]{0:T(128)} %anchor.1, s32[128]{0:T(128)} %valid.1, bf16[16,16,1024]{2,1,0:T(8,128)(2,1)} %x_hbm.1, bf16[1,12,16,2048]{3,2,1,0:T(8,128)(2,1)} %bitcast.6, bf16[1,30,16,1024]{3,2,1,0:T(8,128)(2,1)} %bitcast.5, bf16[1,1024,3072]{2,1,0:T(8,128)(2,1)} %wqkv_hbm.1, ...), custom_call_target="tpu_custom_call" | custom-call | flops 2147483648 | bytes 12582912 | tf_op jit(solution)/shard_map/pallas_call | solution.py:517
  27.0 0.8 %copy.10 = bf16[1,16,16,1024]{3,2,1,0:T(8,128)(2,1)} copy(bf16[1,16,16,1024]{3,2,1,0:T(8,128)(2,1)S(1)} %bitcast.4) | data formatting | bytes 1048576

commit v8 on v4

--- a/solution.py
+++ b/solution.py
@@ -92,7 +92,7 @@
     gone, left = jnp.int32(0), moved
     ranks = []
     for i in range(streams):
-        ranks.append(jnp.where(own_host[i] == me, left, gone))
+        ranks.append(jnp.minimum(jnp.where(own_host[i] == me, left, gone), streams - 1))
         rank[i] = ranks[i]
         left = left + stays[i]
         gone = gone + 1 - stays[i]
@@ -229,15 +229,15 @@
     def conv_kept(chunk):
         def step(w, _):
             at = pl.ds(pl.multiple_of(w * lanes, lanes), lanes)
-            total = jnp.zeros((rows, lanes), jnp.float32)
+            window = [pad_t[chunk, w, t * CHUNK : (t + 1) * CHUNK, :] for t in range(kept_rows)]
+            totals = [None] * frames
             for j in range(kept_rows):
-                n = min(frames, kept_rows - j) * CHUNK
-                term = wconv[j, :, at] * pad_t[chunk, w, pl.ds(j * CHUNK, n), :]
-                if n < rows:
-                    total = jnp.concatenate([total[:n] + term, total[n:]], axis=0)
-                else:
-                    total = total + term
-            conv_t[chunk, w] = total
+                tap = jnp.broadcast_to(wconv[j, :, at], (CHUNK, lanes))
+                for t in range(min(frames, kept_rows - j)):
+                    term = tap * window[t + j]
+                    totals[t] = term if j == 0 else totals[t] + term
+            for t in range(frames):
+                conv_t[chunk, w, t * CHUNK : (t + 1) * CHUNK, :] = totals[t]
             return 0
 
         lax.fori_loop(0, width // lanes, step, 0)
@@ -332,16 +332,19 @@
 
         def conv_new(step, _):
             at = pl.ds(pl.multiple_of(step * lanes, lanes), lanes)
-            total = conv_t[chunk, step]
+            window = [
+                pad_t[chunk, step, (kept_rows + t) * CHUNK : (kept_rows + t + 1) * CHUNK, :]
+                for t in range(frames)
+            ]
+            totals = [conv_t[chunk, step, t * CHUNK : (t + 1) * CHUNK, :] for t in range(frames)]
             for j in range(taps - frames, taps):
-                start = (kept_rows - j) * CHUNK
-                n = rows - start
-                term = wconv[j, :, at] * pad_t[chunk, step, pl.ds(kept_rows * CHUNK, n), :]
-                if start:
-                    total = jnp.concatenate([total[:start], total[start:] + term], axis=0)
-                else:
-                    total = total + term
-            conv_t[chunk, step] = total / (1.0 + jnp.exp(-total))
+                tap = jnp.broadcast_to(wconv[j, :, at], (CHUNK, lanes))
+                first_t = kept_rows - j
+                for t in range(first_t, frames):
+                    totals[t] = totals[t] + tap * window[t - first_t]
+            for t in range(frames):
+                part = 0.5 * totals[t]
+                conv_t[chunk, step, t * CHUNK : (t + 1) * CHUNK, :] = part + part * jnp.tanh(part)
             return 0
 
         lax.fori_loop(0, width // lanes, conv_new, 0)
@@ -449,18 +452,6 @@
         lax.fori_loop(1, hosts, x_sent, 0)
         hand_over(0).wait_send()
         hand_over(1).wait_send()
-
-
-def write_out(held, out_hbm, sem):
-    quarter = held.shape[0] // 4
-    copies = []
-    for i in range(4):
-        span = pl.ds(i * quarter, quarter)
-        copies.append(pltpu.make_async_copy(held.at[span], out_hbm.at[0, span], sem.at[i]))
-    for copy in copies:
-        copy.start()
-    for copy in copies:
-        copy.wait()
 
 
 def body(new_frames, valid, anchor, context, kept, wqkv, wout, wconv):
@@ -535,13 +526,7 @@
         ),
     )
     held = call(anchor, valid, new_frames, context, kept, wqkv, wout, wconv)
-    return pl.pallas_call(
-        write_out,
-        out_shape=jax.ShapeDtypeStruct((1, streams, frames, width), bf16),
-        in_specs=[pl.BlockSpec(memory_space=pltpu.VMEM)],
-        out_specs=pl.BlockSpec(memory_space=pl.ANY),
-        scratch_shapes=[dma((4,))],
-    )(held)
+    return held[None]
 
 
 def solution(mesh):

time: 28.1 us -> 26 us (0.925)
  Pallas kernels: 27.1 us -> 25.1 us
    pallas_call x1 -> x0, Pallas kernels: 1.86 us -> none  [body(): pl.pallas_call(write_out, out_shape=jax.ShapeDtypeStruct((1, streams, fra...]
    unnamed x2 -> x1, local copies, waits for them, and re-layouts: 0.78 us -> 0.8 us
where the time goes in v8:
time: 26 us; the launch traced here: 25.9 us
  Pallas kernels  25.1 us (97%)
  local copies, waits for them, and re-layouts  0.8 us (3%)
    pallas_call x1, Pallas kernels, body(): held = call(anchor, valid, new_frames, context, kept, wqkv, wout, wconv)  25.1 us
    unnamed x1, local copies, waits for them, and re-layouts  0.8 us

profile of v8, /device:TPU:1, one launch (start us, length us, event | category | flops | bytes accessed | tf_op | source)
XLA Modules:
  0.0 25.9 jit_solution(15289435412853101479)
XLA Ops:
  0.0 25.1 %shard_map.82 = bf16[16,16,1024]{2,1,0:T(8,128)(2,1)S(1)} custom-call(s32[128]{0:T(128)} %anchor.1, s32[128]{0:T(128)} %valid.1, bf16[16,16,1024]{2,1,0:T(8,128)(2,1)} %x_hbm.1, bf16[1,12,16,2048]{3,2,1,0:T(8,128)(2,1)} %bitcast.6, bf16[1,30,16,1024]{3,2,1,0:T(8,128)(2,1)} %bitcast.5, bf16[1,1024,3072]{2,1,0:T(8,128)(2,1)} %wqkv_hbm.1, ...), custom_call_target="tpu_custom_call" | custom-call | flops 2147483648 | bytes 12582912 | tf_op jit(solution)/shard_map/pallas_call | solution.py:528
  25.1 0.8 %copy.10 = bf16[1,16,16,1024]{3,2,1,0:T(8,128)(2,1)} copy(bf16[1,16,16,1024]{3,2,1,0:T(8,128)(2,1)S(1)} %bitcast.4) | data formatting | bytes 1048576

commit v9 on v8

--- a/solution.py
+++ b/solution.py
@@ -242,7 +242,8 @@
 
         lax.fori_loop(0, width // lanes, step, 0)
 
-    conv_kept(0)
+    for chunk in range(chunks):
+        conv_kept(chunk)
 
     def project(chunk):
         x = x_work[pl.ds(chunk * CHUNK, CHUNK)].reshape(rows, width).astype(jnp.float32)
@@ -390,7 +391,6 @@
 
     @pl.when(section == 1)
     def _():
-        conv_kept(1)
         hand_over(0).wait_recv()
 
     project(0)
@@ -408,10 +408,6 @@
         return 0
 
     lax.fori_loop(1, hosts, give_back, 0)
-
-    @pl.when(section == 0)
-    def _():
-        conv_kept(1)
 
     @pl.when(section == 1)
     def _():

time: 26 us -> 26 us (level)
  no operation moved by 1% of the time
where the time goes in v9:
time: 26 us; the launch traced here: 25.9 us
  Pallas kernels  25.1 us (97%)
  local copies, waits for them, and re-layouts  0.8 us (3%)
    pallas_call x1, Pallas kernels, body(): held = call(anchor, valid, new_frames, context, kept, wqkv, wout, wconv)  25.1 us
    unnamed x1, local copies, waits for them, and re-layouts  0.8 us

profile of v9, /device:TPU:1, one launch (start us, length us, event | category | flops | bytes accessed | tf_op | source)
XLA Modules:
  0.0 25.9 jit_solution(10656439368231613997)
XLA Ops:
  0.0 25.1 %shard_map.82 = bf16[16,16,1024]{2,1,0:T(8,128)(2,1)S(1)} custom-call(s32[128]{0:T(128)} %anchor.1, s32[128]{0:T(128)} %valid.1, bf16[16,16,1024]{2,1,0:T(8,128)(2,1)} %x_hbm.1, bf16[1,12,16,2048]{3,2,1,0:T(8,128)(2,1)} %bitcast.6, bf16[1,30,16,1024]{3,2,1,0:T(8,128)(2,1)} %bitcast.5, bf16[1,1024,3072]{2,1,0:T(8,128)(2,1)} %wqkv_hbm.1, ...), custom_call_target="tpu_custom_call" | custom-call | flops 2147483648 | bytes 12582912 | tf_op jit(solution)/shard_map/pallas_call | solution.py:524
  25.1 0.8 %copy.10 = bf16[1,16,16,1024]{3,2,1,0:T(8,128)(2,1)} copy(bf16[1,16,16,1024]{3,2,1,0:T(8,128)(2,1)S(1)} %bitcast.4) | data formatting | bytes 1048576
